TPU v7x, 32 devices: a whole 2x2x4 slice. The times are simulated.
32 devices in a mesh: tilt: 4 (over z), pos: 8 (over y, x, core).
Axes of the slice: x: 2, y: 2, z: 4, core: 2. Of those that a mesh axis runs over, the one named last changes fastest.
Arguments:
- intensity: bfloat16 [4, 128, 256, 256], P('tilt', 'pos'), may hold values from 0 to 1
- positions: int32 [4, 128, 2], P('tilt', 'pos'), may hold values from 0 to 512, as said below
- counts: int32 [4, 8], P('tilt', 'pos'), may hold values from 8 to 16, as said below
- object_field: bfloat16 [4, 2, 768, 768], P('tilt', None, 'pos'), may hold values from 0.5 to 1.5
- probe: float32 [2, 256, 256], replicated, may hold values from -3 to 3
Outputs:
- object_grad: float32 [4, 2, 768, 768], P('tilt', None, 'pos')
- probe_grad: float32 [2, 256, 256], replicated
Inputs may be any that keep to these rules, and one draw needn't show every extreme that they name: The batch pairs each flat tilt t < 2 with the steep tilt t + 2: for every position index p, counts[t, p] + counts[t + 2, p] = 24 and counts[t, p] <= 12. `positions`: the row offset of a slot of position index p lies between max(0, (p - 2) * 96) and min(512, (p + 256 // 96 + 1) * 96 - 256); column offsets lie between 0 and 512.
All inputs are finite; a program needn't handle non-finite values.
Results may differ from a plain program's by a relative error of at most 0.0017.
The roundings to bfloat16 on the way count: a program that leaves them out, or rounds other values in their place, can miss the bound.
Values may be sent and summed in bfloat16 or wider, within the bound.
A program may use at most 128 MiB of HBM per device.

v0:
```python
import functools

import jax
import jax.numpy as jnp
import numpy as np
from jax import lax
from jax.experimental import pallas as pl
from jax.experimental.pallas import tpu as pltpu
from jax.sharding import PartitionSpec as P

LANES = 128


def dft_tables(length):
    index = np.arange(length, dtype=np.int64)
    phase = (index[:, None] * index[None, :] % length).astype(np.float64) * (
        2.0 * np.pi / length
    )
    cosine = np.cos(phase) / np.sqrt(length)
    sine = np.sin(phase) / np.sqrt(length)
    forward = np.block([[cosine, -sine], [sine, cosine]])
    inverse = np.block([[cosine, sine], [-sine, cosine]])
    return (
        jnp.asarray(forward.astype(np.float32)).astype(jnp.bfloat16),
        jnp.asarray(inverse.astype(np.float32)).astype(jnp.bfloat16),
    )


def frames_kernel(
    reach,
    pos_ref,
    count_ref,
    frames_ref,
    *refs,
):
    blocks = 2 * reach + 1
    block_refs = refs[:blocks]
    probe_ref, fwd_ref, inv_ref = refs[blocks : blocks + 3]
    out_refs = refs[blocks + 3 : 2 * blocks + 3]
    sums_ref = refs[2 * blocks + 3]
    chunks_ref = sums_ref
    band, total, sums_ref = refs[2 * blocks + 4 :]
    rows = block_refs[0].shape[1]
    groups = block_refs[0].shape[2] // LANES
    width = probe_ref.shape[-1]
    wide = width // LANES

    for b in range(blocks):
        for c in range(2):
            for g in range(groups):
                band[c, g, pl.ds(b * rows, rows), :] = block_refs[b][
                    c, :, g * LANES : (g + 1) * LANES
                ].astype(jnp.float32)
    for c in range(2):
        band[c, groups] = jnp.zeros(band.shape[2:], jnp.float32)
    total[...] = jnp.zeros_like(total)
    sums_ref[...] = jnp.zeros_like(sums_ref)
    first = (lax.axis_index("pos") - reach) * rows

    lane = lax.broadcasted_iota(jnp.int32, (width, LANES), 1)

    def some_frames(at):
        pr, pi = probe_ref[0], probe_ref[1]
        spots, patches, exits = [], [], []
        for i in at:
            r = pos_ref[0, i] - first
            q = pos_ref[1, i]
            qb, qs = q // LANES, lax.rem(q, LANES)
            spots.append((r, qb, qs))
            near = lane < LANES - qs
            back_shift = lax.rem(LANES - qs, LANES)
            patch = []
            for c in range(2):
                rolled = [
                    pltpu.roll(band[c, qb + j, pl.ds(r, width), :], back_shift, 1)
                    for j in range(wide + 1)
                ]
                patch.append(
                    jnp.concatenate(
                        [jnp.where(near, rolled[j], rolled[j + 1]) for j in range(wide)], 1
                    )
                )
            xr, xi = patch
            patches.append((xr, xi))
            exits.append(
                jnp.concatenate(
                    [
                        (pr * xr - pi * xi).astype(jnp.bfloat16),
                        (pr * xi + pi * xr).astype(jnp.bfloat16),
                    ],
                    1,
                )
            )
        halves = jnp.dot(
            jnp.concatenate(exits, 0), fwd_ref[...], preferred_element_type=jnp.float32
        ).astype(jnp.bfloat16)
        mids = []
        for n, i in enumerate(at):
            half = halves[n * width : (n + 1) * width]
            half = jnp.concatenate([half[:, :width], half[:, width:]], 0)
            far = jnp.dot(inv_ref[...], half, preferred_element_type=jnp.float32)
            fr, fi = far[:width], far[width:]
            misfit = fr * fr + fi * fi - frames_ref[i].astype(jnp.float32)
            back = jnp.concatenate(
                [(fr * misfit).astype(jnp.bfloat16), (fi * misfit).astype(jnp.bfloat16)], 0
            )
            mid = jnp.dot(fwd_ref[...], back, preferred_element_type=jnp.float32).astype(
                jnp.bfloat16
            )
            mids.append(jnp.concatenate([mid[:width], mid[width:]], 1))
        waves = jnp.dot(
            jnp.concatenate(mids, 0), inv_ref[...], preferred_element_type=jnp.float32
        )
        sums = [0.0, 0.0, 0.0]
        for n, i in enumerate(at):
            xr, xi = patches[n]
            wave = waves[n * width : (n + 1) * width]
            wr, wi = wave[:, :width], wave[:, width:]
            sums[0] += xr * wr + xi * wi
            sums[1] += xr * wi - xi * wr
            sums[2] += xr * xr + xi * xi
            r, qb, qs = spots[n]
            far_side = lane >= qs
            for c in range(2):
                grad = pr * wr + pi * wi if c == 0 else pr * wi - pi * wr
                grad = grad.astype(jnp.bfloat16).astype(jnp.float32)
                rolled = [
                    pltpu.roll(grad[:, j * LANES : (j + 1) * LANES], qs, 1)
                    for j in range(wide)
                ]
                zero = jnp.zeros_like(rolled[0])
                for j in range(wide + 1):
                    here = rolled[j] if j < wide else zero
                    before = rolled[j - 1] if j > 0 else zero
                    total[c, qb + j, pl.ds(r, width), :] += jnp.where(far_side, here, before)
        for k in range(3):
            sums_ref[k] += sums[k]

    count = count_ref[0, 0]

    @pl.loop(0, count // 2)
    def _(i):
        some_frames([2 * i, 2 * i + 1])

    @pl.when(lax.rem(count, 2) == 1)
    def _():
        some_frames([count - 1])

    for b in range(blocks):
        for c in range(2):
            for g in range(groups):
                out_refs[b][c, :, g * LANES : (g + 1) * LANES] = total[
                    c, g, pl.ds(b * rows, rows), :
                ].astype(out_refs[b].dtype)
    pairs, chips, tilts, _, chunk, _ = chunks_ref.shape
    for e in range(pairs):
        for c in range(chips):
            for t in range(tilts):
                start = ((e * chips + c) * tilts + t) * chunk
                chunks_ref[e, c, t] = sums_ref[:, start : start + chunk, :]


def frame_sums(reach, parts, positions, count, frames, blocks, probe):
    forward, inverse = dft_tables(probe.shape[-1])
    rows, columns = blocks[0].shape[1:]
    groups = columns // LANES
    n = len(blocks)
    vmem = pl.BlockSpec(memory_space=pltpu.VMEM)
    smem = pl.BlockSpec(memory_space=pltpu.SMEM)
    outs = [
        jax.ShapeDtypeStruct(blocks[0].shape, jnp.float32)
        for b in range(n)
    ] + [jax.ShapeDtypeStruct(parts, jnp.float32)]
    return pl.pallas_call(
        functools.partial(frames_kernel, reach),
        out_shape=outs,
        in_specs=[smem, smem, vmem] + [vmem] * (n + 3),
        out_specs=[vmem] * (n + 1),
        scratch_shapes=[
            pltpu.VMEM((2, groups + 1, n * rows, LANES), jnp.float32),
            pltpu.VMEM((2, groups + 1, n * rows, LANES), jnp.float32),
            pltpu.VMEM((3,) + probe.shape[1:], jnp.float32),
        ],
        compiler_params=pltpu.CompilerParams(vmem_limit_bytes=32 * 1024 * 1024),
    )(positions, count, frames, *blocks, probe, forward, inverse)


def greet(tilts, devices):
    t, p = lax.axis_index("tilt"), lax.axis_index("pos")
    barrier = pltpu.get_barrier_semaphore()
    for k in range(1, devices):
        pl.semaphore_signal(
            barrier,
            inc=1,
            device_id=(t, lax.rem(p + k, devices)),
            device_id_type=pl.DeviceIdType.MESH,
        )
    for k in range(1, tilts):
        pl.semaphore_signal(
            barrier,
            inc=1,
            device_id=(lax.rem(t + k, tilts), p),
            device_id_type=pl.DeviceIdType.MESH,
        )
    pl.semaphore_wait(barrier, devices - 1 + tilts - 1)


def send(src, dst, sem_out, sem_in, tilt, pos):
    return pltpu.make_async_remote_copy(
        src_ref=src,
        dst_ref=dst,
        send_sem=sem_out,
        recv_sem=sem_in,
        device_id=(tilt, pos),
        device_id_type=pl.DeviceIdType.MESH,
    )


def gather_kernel(devices, own_ref, *refs):
    slots = {0: refs[0], 1: refs[1], 3: refs[2], 4: refs[3]}
    out_sem, in_sem = refs[4:]
    t, p = lax.axis_index("tilt"), lax.axis_index("pos")
    chip, chips = p // 2, devices // 2
    greet(1, devices)

    def role(odd):
        partner = p - 1 if odd else p + 1

        def copy(src, slot, out, pos):
            return send(src, slots[slot], out_sem.at[out], in_sem.at[slot], t, pos)

        to_partner = copy(own_ref, 3 if odd else 1, 0, partner)
        to_left = copy(own_ref, 4 if odd else 3, 1, 2 * chip - 1)
        to_right = copy(own_ref, 1 if odd else 0, 2, 2 * chip + 2)
        near, far = (3, 4) if odd else (1, 0)
        forward = copy(slots[near], 4 if odd else 0, 3, partner)
        from_partner = 1 if odd else 3
        opposite = 0 if odd else 4
        has_left, has_right = chip > 0, chip < chips - 1
        outer, inner = (has_right, has_left) if odd else (has_left, has_right)

        def arrived(slot):
            copy(own_ref, slot, 0, partner).wait_recv()

        pl.when(has_left)(to_left.start)
        pl.when(has_right)(to_right.start)
        to_partner.start()

        @pl.when(outer)
        def _():
            arrived(near)
            forward.start()
            arrived(far)
            forward.wait_send()

        arrived(from_partner)
        pl.when(inner)(lambda: arrived(opposite))
        pl.when(has_left)(to_left.wait_send)
        pl.when(has_right)(to_right.wait_send)
        to_partner.wait_send()

    pl.when(lax.rem(p, 2) == 0)(lambda: role(False))
    pl.when(lax.rem(p, 2) == 1)(lambda: role(True))


def gather(devices, own):
    vmem = pl.BlockSpec(memory_space=pltpu.VMEM)
    return pl.pallas_call(
        functools.partial(gather_kernel, devices),
        out_shape=[jax.ShapeDtypeStruct(own.shape, own.dtype)] * 4,
        in_specs=[vmem],
        out_specs=[vmem] * 4,
        scratch_shapes=[pltpu.SemaphoreType.DMA((4,)), pltpu.SemaphoreType.DMA((5,))],
        cost_estimate=pl.CostEstimate(
            flops=0, bytes_accessed=64 * 1024 * 1024, transcendentals=0
        ),
        compiler_params=pltpu.CompilerParams(
            collective_id=1, has_side_effects=True, vmem_limit_bytes=4 * 1024 * 1024
        ),
    )(own)


def exchange_kernel(tilts, devices, *refs):
    grads, sums = refs[:5], refs[5]
    object_ref, probe_ref = refs[6:8]
    mine, extra, from_left, from_right, near, distant = refs[8:14]
    half, plane, column, got0, got1, got2, result = refs[14:21]
    obj_out, obj_in, out0, in0, out1, in1, out2, in2, out3, in3, out4, in4, out5, in5 = refs[21:]
    t, p = lax.axis_index("tilt"), lax.axis_index("pos")
    chip, chips = p // 2, devices // 2
    e = lax.rem(p, 2)
    partner = p + 1 - 2 * e
    greet(tilts, devices)

    swap = send(sums.at[1 - e], got0, out0.at[0], in0.at[0], t, partner)

    def objects(odd, step):
        has = chip < chips - 1 if odd else chip > 0
        way = 1 if odd else -1
        lands = from_left if odd else from_right
        slot = 2 if odd else 3
        far = send(distant, lands, obj_out.at[2], obj_in.at[slot], t, p + 2 * way)
        close = send(near, lands, obj_out.at[3], obj_in.at[slot], t, p + way)
        to_extra = send(
            grads[0 if odd else 4], extra, obj_out.at[0], obj_in.at[0], t, partner
        )
        to_mine = send(grads[1 if odd else 3], mine, obj_out.at[1], obj_in.at[1], t, partner)
        if step == 0:
            to_extra.start()
            swap.start()
            distant[...] = grads[4 if odd else 0][...].astype(distant.dtype)
            pl.when(has)(far.start)
            to_mine.start()
        elif step == 1:
            to_extra.wait_recv()
            near[...] = (
                grads[3 if odd else 1][...] + extra[...]
            ).astype(near.dtype)
            pl.when(has)(close.start)
        else:
            to_mine.wait_recv()
            to_extra.wait_send()
            to_mine.wait_send()

            @pl.when(has)
            def _():
                far.wait_send()
                close.wait_send()

    def both(step):
        pl.when(e == 0)(lambda: objects(False, step))
        pl.when(e == 1)(lambda: objects(True, step))

    both(0)
    swap.wait_recv()
    half[...] = sums[e] + got0[...]
    round1 = []
    for k in range(1, chips):
        other = lax.rem(chip + k, chips)
        round1.append(
            send(half.at[other], got1.at[k - 1], out1.at[k - 1], in1.at[k - 1], t, 2 * other + e)
        )
        round1[-1].start()
    both(1)
    total = half[chip]
    for k in range(1, chips):
        round1[k - 1].wait_recv()
        total = total + got1[k - 1]
    plane[...] = total
    round2 = []
    for k in range(1, tilts):
        other = lax.rem(t + k, tilts)
        round2.append(
            send(plane.at[other], got2.at[k - 1], out2.at[k - 1], in2.at[k - 1], other, p)
        )
        round2[-1].start()
    total = plane[t]
    for k in range(1, tilts):
        round2[k - 1].wait_recv()
        total = total + got2[k - 1]
    column[...] = total[:2] / total[2:]
    result[e, chip, t] = column[...]
    round3 = []
    for k in range(1, tilts):
        other = lax.rem(t + k, tilts)
        round3.append(
            send(column, result.at[e, chip, t], out3.at[k - 1], in3.at[k - 1], other, p)
        )
        round3[-1].start()
    for k in range(1, tilts):
        round3[k - 1].wait_recv()
    round4 = []
    for k in range(1, chips):
        other = lax.rem(chip + k, chips)
        round4.append(
            send(
                result.at[e, chip],
                result.at[e, chip],
                out4.at[k - 1],
                in4.at[k - 1],
                t,
                2 * other + e,
            )
        )
        round4[-1].start()
    for k in range(1, chips):
        round4[k - 1].wait_recv()
    back = send(result.at[e], result.at[e], out5.at[0], in5.at[0], t, partner)
    back.start()

    both(2)
    object_ref[0] = grads[2][...] + mine[...]

    @pl.when(chip > 0)
    def _():
        send(near, from_left, obj_out.at[3], obj_in.at[2], t, partner).wait_recv()
        object_ref[0] += from_left[...].astype(jnp.float32)

    @pl.when(chip < chips - 1)
    def _():
        send(near, from_right, obj_out.at[3], obj_in.at[3], t, partner).wait_recv()
        object_ref[0] += from_right[...].astype(jnp.float32)

    back.wait_recv()
    chunk = result.shape[-2]
    for i in range(2):
        for c in range(chips):
            for s in range(tilts):
                start = ((i * chips + c) * tilts + s) * chunk
                probe_ref[:, start : start + chunk, :] = result[i, c, s]
    swap.wait_send()
    for copy in round1 + round2 + round3 + round4:
        copy.wait_send()
    back.wait_send()


def exchange(tilts, devices, grads, sums):
    vmem = pl.BlockSpec(memory_space=pltpu.VMEM)
    _, chips, _, planes, chunk, width = sums.shape
    block = grads[0].shape
    dma = pltpu.SemaphoreType.DMA
    f32 = jnp.float32
    return pl.pallas_call(
        functools.partial(exchange_kernel, tilts, devices),
        out_shape=[
            jax.ShapeDtypeStruct((1,) + block, f32),
            jax.ShapeDtypeStruct((2, width, width), f32),
        ],
        in_specs=[vmem] * 6,
        out_specs=[vmem] * 2,
        scratch_shapes=[pltpu.VMEM(block, f32)] * 2
        + [pltpu.VMEM(block, jnp.bfloat16)] * 4
        + [
            pltpu.VMEM((chips, tilts, planes, chunk, width), f32),
            pltpu.VMEM((tilts, planes, chunk, width), f32),
            pltpu.VMEM((2, chunk, width), f32),
            pltpu.VMEM((chips, tilts, planes, chunk, width), f32),
            pltpu.VMEM((chips - 1, tilts, planes, chunk, width), f32),
            pltpu.VMEM((tilts - 1, planes, chunk, width), f32),
            pltpu.VMEM((2, chips, tilts, 2, chunk, width), f32),
        ]
        + [dma((4,)), dma((4,))]
        + [dma((1,))] * 2
        + [dma((chips - 1,))] * 2
        + [dma((tilts - 1,))] * 4
        + [dma((chips - 1,))] * 2
        + [dma((1,))] * 2,
        compiler_params=pltpu.CompilerParams(
            collective_id=2, has_side_effects=True, vmem_limit_bytes=20 * 1024 * 1024
        ),
    )(*grads, sums)


def local(tilts, devices, intensity, positions, counts, object_field, probe):
    width = probe.shape[-1]
    rows = object_field.shape[2]
    reach = width // rows
    assert reach == 2 and devices % 2 == 0
    own = object_field[0]
    left2, left1, right1, right2 = gather(devices, own)
    blocks = [left2, left1, own, right1, right2]
    parts = (2, devices // 2, tilts, 3, width // (devices * tilts), width)
    *grads, sums = frame_sums(reach, parts, positions[0].T, counts, intensity[0], blocks, probe)
    return tuple(exchange(tilts, devices, grads, sums))


def solution(mesh):
    placed = (
        P("tilt", "pos", None, None),
        P("tilt", "pos", None),
        P("tilt", "pos"),
        P("tilt", None, "pos", None),
        P(),
    )
    return jax.shard_map(
        functools.partial(local, mesh.shape["tilt"], mesh.shape["pos"]),
        mesh=mesh,
        in_specs=placed,
        out_specs=(P("tilt", None, "pos", None), P()),
        check_vma=False,
    )
```

profile of v0, /device:TPU:0, one launch (start us, length us, event | category | flops | bytes accessed | tf_op | source)
XLA Modules:
  0.0 81.0 jit_solution(9538341642212304934)
XLA Ops:
  1.3 0.0 copy-start.1
  1.3 1.0 %copy-done.1 = bf16[1,2,96,768]{3,2,1,0:T(8,128)(2,1)S(1)} copy-done((bf16[1,2,96,768]{3,2,1,0:T(8,128)(2,1)S(1)}, bf16[1,2,96,768]{3,2,1,0:T(8,128)(2,1)}, u32[]{:S(2)}) %copy-start.1) | copy-done | bytes 294936
  2.2 13.2 %shard_map.86 = (bf16[2,96,768]{2,1,0:T(8,128)(2,1)S(1)}, bf16[2,96,768]{2,1,0:T(8,128)(2,1)S(1)}, bf16[2,96,768]{2,1,0:T(8,128)(2,1)S(1)}, bf16[2,96,768]{2,1,0:T(8,128)(2,1)S(1)}) custom-call(bf16[2,96,768]{2,1,0:T(8,128)(2,1)S(1)} %bitcast.6), custom_call_target="tpu_custom_call" | custom-call | bytes 67108864 | tf_op jit(solution)/shard_map/pallas_call | solution.py:268
  15.5 0.0 copy-start
  15.5 1.6 %copy-done = bf16[1,16,256,256]{3,2,1,0:T(8,128)(2,1)S(1)} copy-done((bf16[1,16,256,256]{3,2,1,0:T(8,128)(2,1)S(1)}, bf16[1,16,256,256]{3,2,1,0:T(8,128)(2,1)}, u32[]{:S(2)}) %copy-start) | copy-done | bytes 2097176
  17.1 0.0 copy-start.2
  17.1 1.0 %copy-done.2 = bf16[1,2,96,768]{3,2,1,0:T(8,128)(2,1)S(1)} copy-done((bf16[1,2,96,768]{3,2,1,0:T(8,128)(2,1)S(1)}, bf16[1,2,96,768]{3,2,1,0:T(8,128)(2,1)}, u32[]{:S(2)}) %copy-start.2) | copy-done | bytes 294936
  18.0 0.0 copy-start.3
  18.0 1.0 %copy-done.3 = f32[2,256,256]{2,1,0:T(8,128)S(1)} copy-done((f32[2,256,256]{2,1,0:T(8,128)S(1)}, f32[2,256,256]{2,1,0:T(8,128)}, u32[]{:S(2)}) %copy-start.3) | copy-done | bytes 524312
  19.1 0.0 copy-start.4
  19.1 1.0 %copy-done.4 = bf16[512,512]{1,0:T(8,128)(2,1)S(1)} copy-done((bf16[512,512]{1,0:T(8,128)(2,1)S(1)}, bf16[512,512]{1,0:T(8,128)(2,1)}, u32[]{:S(2)}) %copy-start.4) | copy-done | bytes 524312
  20.1 0.0 copy-start.5
  20.1 1.0 %copy-done.5 = bf16[512,512]{1,0:T(8,128)(2,1)S(1)} copy-done((bf16[512,512]{1,0:T(8,128)(2,1)S(1)}, bf16[512,512]{1,0:T(8,128)(2,1)}, u32[]{:S(2)}) %copy-start.5) | copy-done | bytes 524312
  21.2 0.0 copy-start.6
  21.2 0.7 copy-done.6
  21.8 11.5 %shard_map.87 = (f32[2,96,768]{2,1,0:T(8,128)S(1)}, f32[2,96,768]{2,1,0:T(8,128)S(1)}, f32[2,96,768]{2,1,0:T(8,128)S(1)}, f32[2,96,768]{2,1,0:T(8,128)S(1)}, f32...) custom-call(s32[2,16]{1,0:T(2,128)S(1)} %bitcast.8, s32[1,1]{1,0:T(1,128)S(6)} %copy.11.count_ref, ...), custom_call_target="tpu_custom_call" | custom-call | tf_op jit(solution)/shard_map/pallas_call | solution.py:174
  33.4 46.0 %shard_map.88 = (f32[1,2,96,768]{3,2,1,0:T(8,128)S(1)}, f32[2,256,256]{2,1,0:T(8,128)S(1)}) custom-call(f32[2,96,768]{2,1,0:T(8,128)S(1)} %get-tuple-element.16.refs_0_, f32[2,96,768]{2,1,0:T(8,128)S(1)} %get-tuple-element.17.refs_1_, f32[2,96,768]{2,1,0:T(8,128)S(1)} %get-tuple-element.18.refs_2_, f32[2,96,768]{2,1,0:T(8,128)S(1)} %get-tuple-element.19.refs_3_, ...), custom_call_target="tpu_custom_call" | custom-call | tf_op jit(solution)/shard_map/pallas_call | solution.py:423
  79.3 0.8 %copy.12 = f32[1,2,96,768]{3,2,1,0:T(8,128)} copy(f32[1,2,96,768]{3,2,1,0:T(8,128)S(1)} %get-tuple-element.24) | data formatting | bytes 1179648
  80.2 0.8 copy.13
Async XLA Ops:
  1.3 1.0 %copy-start.1 = (bf16[1,2,96,768]{3,2,1,0:T(8,128)(2,1)S(1)}, bf16[1,2,96,768]{3,2,1,0:T(8,128)(2,1)}, u32[]{:S(2)}) copy-start(bf16[1,2,96,768]{3,2,1,0:T(8,128)(2,1)} %param.10) | copy-start | bytes 884740
  15.5 1.6 %copy-start = (bf16[1,16,256,256]{3,2,1,0:T(8,128)(2,1)S(1)}, bf16[1,16,256,256]{3,2,1,0:T(8,128)(2,1)}, u32[]{:S(2)}) copy-start(bf16[1,16,256,256]{3,2,1,0:T(8,128)(2,1)} %param.7) | copy-start | bytes 6291460
  17.1 1.0 %copy-start.2 = (bf16[1,2,96,768]{3,2,1,0:T(8,128)(2,1)S(1)}, bf16[1,2,96,768]{3,2,1,0:T(8,128)(2,1)}, u32[]{:S(2)}) copy-start(bf16[1,2,96,768]{3,2,1,0:T(8,128)(2,1)} %param.10) | copy-start | bytes 884740
  18.0 1.0 %copy-start.3 = (f32[2,256,256]{2,1,0:T(8,128)S(1)}, f32[2,256,256]{2,1,0:T(8,128)}, u32[]{:S(2)}) copy-start(f32[2,256,256]{2,1,0:T(8,128)} %refs_5_.1) | copy-start | bytes 1572868
  19.1 1.0 %copy-start.4 = (bf16[512,512]{1,0:T(8,128)(2,1)S(1)}, bf16[512,512]{1,0:T(8,128)(2,1)}, u32[]{:S(2)}) copy-start(bf16[512,512]{1,0:T(8,128)(2,1)} %constant.11.refs_7_) | copy-start | bytes 1572868
  20.1 1.0 %copy-start.5 = (bf16[512,512]{1,0:T(8,128)(2,1)S(1)}, bf16[512,512]{1,0:T(8,128)(2,1)}, u32[]{:S(2)}) copy-start(bf16[512,512]{1,0:T(8,128)(2,1)} %constant.10.refs_6_) | copy-start | bytes 1572868
  21.2 0.7 copy-start.6
where the time goes:
time: 81.4 us; the launch traced here: 81 us
  Pallas kernels  70.7 us (87%)
  local copies, waits for them, and re-layouts  8.92 us (11%)
  between operations  1.32 us (2%)
    pallas_call x1, Pallas kernels, exchange(): pl.pallas_call(functools.partial(exchange_kernel, tilts, devices), out_sh...  46 us
    pallas_call x1, Pallas kernels, gather(): pl.pallas_call(functools.partial(gather_kernel, devices), out_shape=[jax....  13.2 us
    pallas_call x1, Pallas kernels, frame_sums(): pl.pallas_call(functools.partial(frames_kernel, reach), out_shape=outs, i...  11.5 us
    unnamed x16, local copies, waits for them, and re-layouts  8.92 us

commit v1 on v0

v1 whole, which is shorter than its diff:
```python
import functools

import jax
import jax.numpy as jnp
import numpy as np
from jax import lax
from jax.experimental import pallas as pl
from jax.experimental.pallas import tpu as pltpu
from jax.sharding import PartitionSpec as P

LANES = 128


def dft_tables(length):
    index = np.arange(length, dtype=np.int64)
    phase = (index[:, None] * index[None, :] % length).astype(np.float64) * (
        2.0 * np.pi / length
    )
    cosine = np.cos(phase) / np.sqrt(length)
    sine = np.sin(phase) / np.sqrt(length)
    forward = np.block([[cosine, -sine], [sine, cosine]])
    inverse = np.block([[cosine, sine], [-sine, cosine]])
    return (
        jnp.asarray(forward.astype(np.float32)).astype(jnp.bfloat16),
        jnp.asarray(inverse.astype(np.float32)).astype(jnp.bfloat16),
    )


def frames_kernel(
    reach,
    tilts,
    pos_any,
    count_ref,
    frames_ref,
    band,
    probe_ref,
    fwd_ref,
    inv_ref,
    total,
    chunks_ref,
    sums_ref,
    pos_ref,
    pos_sem,
):
    fetch = pltpu.make_async_copy(pos_any, pos_ref, pos_sem)
    fetch.start()
    rows = band.shape[2] // (2 * reach + 1)
    width = probe_ref.shape[-1]
    wide = width // LANES

    total[...] = jnp.zeros_like(total)
    sums_ref[...] = jnp.zeros_like(sums_ref)
    first = (lax.axis_index("pos") - reach) * rows
    fetch.wait()

    lane = lax.broadcasted_iota(jnp.int32, (width, LANES), 1)

    def some_frames(at):
        pr, pi = probe_ref[0], probe_ref[1]
        spots, patches, exits = [], [], []
        for i in at:
            r = pos_ref[0, i] - first
            q = pos_ref[1, i]
            qb, qs = q // LANES, lax.rem(q, LANES)
            spots.append((r, qb, qs))
            near = lane < LANES - qs
            back_shift = lax.rem(LANES - qs, LANES)
            patch = []
            for c in range(2):
                rolled = [
                    pltpu.roll(band[c, qb + j, pl.ds(r, width), :], back_shift, 1)
                    for j in range(wide + 1)
                ]
                patch.append(
                    jnp.concatenate(
                        [jnp.where(near, rolled[j], rolled[j + 1]) for j in range(wide)], 1
                    )
                )
            xr, xi = patch
            patches.append((xr, xi))
            exits.append(
                jnp.concatenate(
                    [
                        (pr * xr - pi * xi).astype(jnp.bfloat16),
                        (pr * xi + pi * xr).astype(jnp.bfloat16),
                    ],
                    1,
                )
            )
        halves = jnp.dot(
            jnp.concatenate(exits, 0), fwd_ref[...], preferred_element_type=jnp.float32
        ).astype(jnp.bfloat16)
        mids = []
        for n, i in enumerate(at):
            half = halves[n * width : (n + 1) * width]
            half = jnp.concatenate([half[:, :width], half[:, width:]], 0)
            far = jnp.dot(inv_ref[...], half, preferred_element_type=jnp.float32)
            fr, fi = far[:width], far[width:]
            misfit = fr * fr + fi * fi - frames_ref[i].astype(jnp.float32)
            back = jnp.concatenate(
                [(fr * misfit).astype(jnp.bfloat16), (fi * misfit).astype(jnp.bfloat16)], 0
            )
            mid = jnp.dot(fwd_ref[...], back, preferred_element_type=jnp.float32).astype(
                jnp.bfloat16
            )
            mids.append(jnp.concatenate([mid[:width], mid[width:]], 1))
        waves = jnp.dot(
            jnp.concatenate(mids, 0), inv_ref[...], preferred_element_type=jnp.float32
        )
        sums = [0.0, 0.0, 0.0]
        for n, i in enumerate(at):
            xr, xi = patches[n]
            wave = waves[n * width : (n + 1) * width]
            wr, wi = wave[:, :width], wave[:, width:]
            sums[0] += xr * wr + xi * wi
            sums[1] += xr * wi - xi * wr
            sums[2] += xr * xr + xi * xi
            r, qb, qs = spots[n]
            far_side = lane >= qs
            for c in range(2):
                grad = pr * wr + pi * wi if c == 0 else pr * wi - pi * wr
                grad = grad.astype(jnp.bfloat16).astype(jnp.float32)
                rolled = [
                    pltpu.roll(grad[:, j * LANES : (j + 1) * LANES], qs, 1)
                    for j in range(wide)
                ]
                zero = jnp.zeros_like(rolled[0])
                for j in range(wide + 1):
                    here = rolled[j] if j < wide else zero
                    before = rolled[j - 1] if j > 0 else zero
                    total[c, qb + j, pl.ds(r, width), :] += jnp.where(far_side, here, before)
        for k in range(3):
            sums_ref[k] += sums[k]

    count = count_ref[0, 0]

    @pl.loop(0, count // 2)
    def _(i):
        some_frames([2 * i, 2 * i + 1])

    @pl.when(lax.rem(count, 2) == 1)
    def _():
        some_frames([count - 1])

    pairs, chips, _, _ = chunks_ref.shape
    chunk = chunks_ref.shape[2] // (3 * tilts)
    for e in range(pairs):
        for c in range(chips):
            for t in range(tilts):
                start = ((e * chips + c) * tilts + t) * chunk
                for k in range(3):
                    chunks_ref[e, c, pl.ds((t * 3 + k) * chunk, chunk), :] = sums_ref[
                        k, start : start + chunk, :
                    ]


def frame_sums(reach, tilts, parts, positions, count, frames, band, probe, forward, inverse):
    vmem = pl.BlockSpec(memory_space=pltpu.VMEM)
    smem = pl.BlockSpec(memory_space=pltpu.SMEM)
    return pl.pallas_call(
        functools.partial(frames_kernel, reach, tilts),
        out_shape=[
            jax.ShapeDtypeStruct(band.shape, jnp.float32),
            jax.ShapeDtypeStruct(parts, jnp.float32),
        ],
        in_specs=[vmem, smem] + [vmem] * 5,
        out_specs=[vmem] * 2,
        scratch_shapes=[
            pltpu.VMEM((3,) + probe.shape[1:], jnp.float32),
            pltpu.SMEM(positions.shape, jnp.int32),
            pltpu.SemaphoreType.DMA,
        ],
        compiler_params=pltpu.CompilerParams(vmem_limit_bytes=24 * 1024 * 1024),
    )(positions, count, frames, band, probe, forward, inverse)


def greet(tilts, devices):
    t, p = lax.axis_index("tilt"), lax.axis_index("pos")
    barrier = pltpu.get_barrier_semaphore()
    for k in range(1, devices):
        pl.semaphore_signal(
            barrier,
            inc=1,
            device_id=(t, lax.rem(p + k, devices)),
            device_id_type=pl.DeviceIdType.MESH,
        )
    for k in range(1, tilts):
        pl.semaphore_signal(
            barrier,
            inc=1,
            device_id=(lax.rem(t + k, tilts), p),
            device_id_type=pl.DeviceIdType.MESH,
        )
    pl.semaphore_wait(barrier, devices - 1 + tilts - 1)


def send(src, dst, sem_out, sem_in, tilt, pos):
    return pltpu.make_async_remote_copy(
        src_ref=src,
        dst_ref=dst,
        send_sem=sem_out,
        recv_sem=sem_in,
        device_id=(tilt, pos),
        device_id_type=pl.DeviceIdType.MESH,
    )


def relayed(devices):
    return devices == 8


def gather_kernel(
    devices,
    field_any,
    frames_any,
    probe_any,
    fwd_any,
    inv_any,
    pos_any,
    band,
    frames_ref,
    probe_ref,
    fwd_ref,
    inv_ref,
    pos_ref,
    own,
    slots,
    stage,
    out_sem,
    in_sem,
    relay_out,
    relay_in,
    local_sem,
):
    t, p = lax.axis_index("tilt"), lax.axis_index("pos")
    chip, chips = p // 2, devices // 2
    rows = own.shape[1]
    groups = own.shape[2] // LANES

    own_copy = pltpu.make_async_copy(field_any.at[0], own, local_sem.at[0])
    own_copy.start()
    loads = [
        pltpu.make_async_copy(src, dst, local_sem.at[1 + n])
        for n, (src, dst) in enumerate(
            [
                (pos_any, pos_ref),
                (probe_any, probe_ref),
                (fwd_any, fwd_ref),
                (inv_any, inv_ref),
                (frames_any.at[0], frames_ref),
            ]
        )
    ]
    greet(1, devices)
    own_copy.wait()

    def place(src, b):
        for c in range(2):
            for g in range(groups):
                band[c, g, pl.ds(b * rows, rows), :] = src[
                    c, :, g * LANES : (g + 1) * LANES
                ].astype(jnp.float32)

    def role(odd):
        partner = p - 1 if odd else p + 1
        has_left, has_right = chip > 0, chip < chips - 1
        near, far = (3, 4) if odd else (1, 0)
        onward = 4 if odd else 0
        from_partner = 1 if odd else 3
        opposite = 0 if odd else 4
        outer, inner = (has_right, has_left) if odd else (has_left, has_right)
        slot_left, slot_right = (4, 1) if odd else (3, 0)
        pos_left, pos_right = 2 * chip - 1, 2 * chip + 2

        def copy(src, slot, c, out, pos):
            return send(
                src.at[c], slots.at[slot, c], out_sem.at[out, c], in_sem.at[slot, c], t, pos
            )

        to_left = [copy(own, slot_left, c, 1, pos_left) for c in range(2)]
        to_right = [copy(own, slot_right, c, 2, pos_right) for c in range(2)]
        to_partner = [copy(own, 3 if odd else 1, c, 0, partner) for c in range(2)]
        forward = [copy(slots.at[near], onward, c, 3, partner) for c in range(2)]

        def arrived(slot, c):
            copy(own, slot, c, 0, partner).wait_recv()

        if relayed(devices):
            across = lax.rem(p + 4, 8)
            to_stage = send(own.at[1], stage, relay_out.at[0], relay_in.at[0], t, across)
            staged_right = send(
                stage, slots.at[slot_right, 1], relay_out.at[1], in_sem.at[slot_right, 1], t, 4
            )
            staged_left = send(
                stage, slots.at[slot_left, 1], relay_out.at[2], in_sem.at[slot_left, 1], t, 3
            )
            middle = (chip == 1) | (chip == 2)
            pl.when(middle)(to_stage.start)
            pl.when(has_left)(to_left[0].start)
            pl.when(has_right)(to_right[0].start)
            pl.when(has_left & (chip != 2))(to_left[1].start)
            pl.when(has_right & (chip != 1))(to_right[1].start)
        else:
            for c in range(2):
                pl.when(has_left)(to_left[c].start)
                pl.when(has_right)(to_right[c].start)
        for c in range(2):
            to_partner[c].start()
        for load in loads:
            load.start()
        for c in range(2):
            band[c, groups] = jnp.zeros(band.shape[2:], jnp.float32)
        place(own, 2)
        for c in range(2):
            arrived(from_partner, c)
        place(slots.at[from_partner], from_partner)
        if relayed(devices):

            @pl.when(chip == 0)
            def _():
                to_stage.wait_recv()
                staged_left.start()

            @pl.when(chip == 3)
            def _():
                to_stage.wait_recv()
                staged_right.start()

        @pl.when(outer)
        def _():
            for c in range(2):
                arrived(near, c)
                forward[c].start()
            place(slots.at[near], near)
            for c in range(2):
                arrived(far, c)
            place(slots.at[far], far)

        @pl.when(inner)
        def _():
            for c in range(2):
                arrived(opposite, c)
            place(slots.at[opposite], opposite)

        for load in loads:
            load.wait()
        pl.when(has_left)(to_left[0].wait_send)
        pl.when(has_right)(to_right[0].wait_send)
        if relayed(devices):
            pl.when(middle)(to_stage.wait_send)
            pl.when(has_left & (chip != 2))(to_left[1].wait_send)
            pl.when(has_right & (chip != 1))(to_right[1].wait_send)
            pl.when(chip == 0)(staged_left.wait_send)
            pl.when(chip == 3)(staged_right.wait_send)
        else:
            pl.when(has_left)(to_left[1].wait_send)
            pl.when(has_right)(to_right[1].wait_send)
        for c in range(2):
            to_partner[c].wait_send()
            pl.when(outer)(forward[c].wait_send)

    pl.when(lax.rem(p, 2) == 0)(lambda: role(False))
    pl.when(lax.rem(p, 2) == 1)(lambda: role(True))


def gather(devices, field, frames, probe, forward, inverse, positions):
    hbm = pl.BlockSpec(memory_space=pltpu.HBM)
    vmem = pl.BlockSpec(memory_space=pltpu.VMEM)
    _, planes, rows, columns = field.shape
    block = (planes, rows, columns)
    groups = columns // LANES
    dma = pltpu.SemaphoreType.DMA
    return pl.pallas_call(
        functools.partial(gather_kernel, devices),
        out_shape=[
            jax.ShapeDtypeStruct((planes, groups + 1, 5 * rows, LANES), jnp.float32),
            jax.ShapeDtypeStruct(frames.shape[1:], frames.dtype),
            jax.ShapeDtypeStruct(probe.shape, probe.dtype),
            jax.ShapeDtypeStruct(forward.shape, forward.dtype),
            jax.ShapeDtypeStruct(inverse.shape, inverse.dtype),
            jax.ShapeDtypeStruct(positions.shape, positions.dtype),
        ],
        in_specs=[hbm] * 6,
        out_specs=[vmem] * 6,
        scratch_shapes=[
            pltpu.VMEM(block, field.dtype),
            pltpu.VMEM((5,) + block, field.dtype),
            pltpu.VMEM((rows, columns), field.dtype),
            dma((4, 2)),
            dma((5, 2)),
            dma((3,)),
            dma((1,)),
            dma((6,)),
        ],
        compiler_params=pltpu.CompilerParams(
            collective_id=1, has_side_effects=True, vmem_limit_bytes=16 * 1024 * 1024
        ),
    )(field, frames, probe, forward, inverse, positions)


def exchange_kernel(tilts, devices, *refs):
    grads, sums, object_ref, probe_ref = refs[:4]
    mine, extra, from_left, from_right, near, distant, stage = refs[4:11]
    half, got0, got1, plane, column, got2, result = refs[11:18]
    obj_out, obj_in, stage_out, stage_in = refs[18:22]
    out0, in0, out1, in1, out2, in2, out3, in3, out4, in4, out5, in5 = refs[22:]
    t, p = lax.axis_index("tilt"), lax.axis_index("pos")
    chip, chips = p // 2, devices // 2
    e = lax.rem(p, 2)
    partner = p + 1 - 2 * e
    groups, rows = mine.shape[1:3]
    chunk = column.shape[0] // 2
    relay = relayed(devices)
    greet(tilts, devices)

    def block(b):
        return grads.at[:, pl.ds(0, groups), pl.ds(b * rows, rows), :]

    swap = send(sums.at[1 - e], got0, out0.at[0], in0.at[0], t, partner)

    def objects(odd, step):
        has = chip < chips - 1 if odd else chip > 0
        way = 1 if odd else -1
        middle = (chip == 1) if odd else (chip == 2)
        corner = (chip == 3) if odd else (chip == 0)
        lands = from_left if odd else from_right
        side = 0 if odd else 1
        across = lax.rem(p + 4, 8)

        def out(src, n, c, pos):
            return send(src.at[c], lands.at[c], obj_out.at[n, c], obj_in.at[side, c], t, pos)

        far = [out(distant, 0, c, p + 2 * way) for c in range(2)]
        close = [out(near, 1, c, p + way) for c in range(2)]
        to_extra = send(
            block(0 if odd else 4), extra, obj_out.at[2, 0], obj_in.at[2, 0], t, partner
        )
        to_mine = send(block(1 if odd else 3), mine, obj_out.at[2, 1], obj_in.at[2, 1], t, partner)
        if relay:
            up = [
                send(src.at[1], stage.at[n], stage_out.at[n], stage_in.at[n], t, across)
                for n, src in enumerate([distant, near])
            ]
            onto = [(5, 4), (2, 3)][side]
            on = [
                send(stage.at[n], lands.at[1], stage_out.at[2 + n], obj_in.at[side, 1], t, onto[n])
                for n in range(2)
            ]
        if step == 0:
            to_extra.start()
            b = 4 if odd else 0
            for c in range(2):
                distant[c] = grads[c, 0:groups, pl.ds(b * rows, rows), :].astype(distant.dtype)
            pl.when(has)(far[0].start)
            if relay:
                pl.when(middle)(up[0].start)
        elif step == 1:
            if relay:
                pl.when(has & ~middle)(far[1].start)
            else:
                pl.when(has)(far[1].start)
            to_mine.start()
            to_extra.wait_recv()
            b = 3 if odd else 1
            for c in range(2):
                near[c] = (
                    grads[c, 0:groups, pl.ds(b * rows, rows), :] + extra[c]
                ).astype(near.dtype)
            pl.when(has)(close[0].start)
            if relay:
                pl.when(middle)(up[1].start)
                pl.when(has & ~middle)(close[1].start)

                @pl.when(corner)
                def _():
                    up[0].wait_recv()
                    on[0].start()
            else:
                pl.when(has)(close[1].start)
        elif step == 2:
            if relay:

                @pl.when(corner)
                def _():
                    up[1].wait_recv()
                    on[1].start()
        else:
            to_mine.wait_recv()
            to_extra.wait_send()
            to_mine.wait_send()
            pl.when(has)(far[0].wait_send)
            pl.when(has)(close[0].wait_send)
            if relay:
                for n, direct in enumerate([far[1], close[1]]):
                    pl.when(has & ~middle)(direct.wait_send)
                    pl.when(middle)(up[n].wait_send)
                    pl.when(corner)(on[n].wait_send)
            else:
                pl.when(has)(far[1].wait_send)
                pl.when(has)(close[1].wait_send)

    def both(step):
        pl.when(e == 0)(lambda: objects(False, step))
        pl.when(e == 1)(lambda: objects(True, step))

    swap.start()
    both(0)
    swap.wait_recv()
    half[...] = (sums[e] + got0[...]).astype(half.dtype)
    round1 = []
    for k in range(1, chips):
        other = lax.rem(chip + k, chips)
        round1.append(
            send(half.at[other], got1.at[k - 1], out1.at[k - 1], in1.at[k - 1], t, 2 * other + e)
        )
        round1[-1].start()
    both(1)
    total = sums[e, chip] + got0[chip]
    for k in range(1, chips):
        round1[k - 1].wait_recv()
        total = total + got1[k - 1].astype(jnp.float32)
    for s in range(tilts):
        plane[s] = total[s * 3 * chunk : (s + 1) * 3 * chunk]
    round2 = []
    for k in range(1, tilts):
        other = lax.rem(t + k, tilts)
        round2.append(
            send(plane.at[other], got2.at[k - 1], out2.at[k - 1], in2.at[k - 1], other, p)
        )
        round2[-1].start()
    both(2)
    total = plane[t]
    for k in range(1, tilts):
        round2[k - 1].wait_recv()
        total = total + got2[k - 1]
    below = total[2 * chunk :]
    column[...] = total[: 2 * chunk] / jnp.concatenate([below, below], 0)
    result[e, chip, t] = column[...]
    round3 = []
    for k in range(1, tilts):
        other = lax.rem(t + k, tilts)
        round3.append(
            send(column, result.at[e, chip, t], out3.at[k - 1], in3.at[k - 1], other, p)
        )
        round3[-1].start()
    for k in range(1, tilts):
        round3[k - 1].wait_recv()
    round4 = []
    for k in range(1, chips):
        other = lax.rem(chip + k, chips)
        round4.append(
            send(
                result.at[e, chip],
                result.at[e, chip],
                out4.at[k - 1],
                in4.at[k - 1],
                t,
                2 * other + e,
            )
        )
        round4[-1].start()
    for k in range(1, chips):
        round4[k - 1].wait_recv()
    back = send(result.at[e], result.at[e], out5.at[0], in5.at[0], t, partner)
    back.start()

    both(3)
    for c in range(2):
        for g in range(groups):
            object_ref[0, c, :, g * LANES : (g + 1) * LANES] = (
                grads[c, g, pl.ds(2 * rows, rows), :] + mine[c, g]
            )
    for side, has, landed in [(0, chip > 0, from_left), (1, chip < chips - 1, from_right)]:

        @pl.when(has)
        def _():
            for c in range(2):
                send(
                    near.at[c], landed.at[c], obj_out.at[1, c], obj_in.at[side, c], t, partner
                ).wait_recv()
                for g in range(groups):
                    object_ref[0, c, :, g * LANES : (g + 1) * LANES] += landed[c, g].astype(
                        jnp.float32
                    )

    back.wait_recv()
    for i in range(2):
        for c in range(chips):
            for s in range(tilts):
                start = ((i * chips + c) * tilts + s) * chunk
                for k in range(2):
                    probe_ref[k, start : start + chunk, :] = result[
                        i, c, s, k * chunk : (k + 1) * chunk, :
                    ]
    swap.wait_send()
    for copy in round1 + round2 + round3 + round4:
        copy.wait_send()
    back.wait_send()


def exchange(tilts, devices, width, rows, grads, sums):
    vmem = pl.BlockSpec(memory_space=pltpu.VMEM)
    planes, groups = grads.shape[0], grads.shape[1] - 1
    _, chips, part, _ = sums.shape
    third = part // tilts
    block = (planes, groups, rows, LANES)
    dma = pltpu.SemaphoreType.DMA
    f32, bf16 = jnp.float32, jnp.bfloat16
    return pl.pallas_call(
        functools.partial(exchange_kernel, tilts, devices),
        out_shape=[
            jax.ShapeDtypeStruct((1, planes, rows, groups * LANES), f32),
            jax.ShapeDtypeStruct((2, width, width), f32),
        ],
        in_specs=[vmem] * 2,
        out_specs=[vmem] * 2,
        scratch_shapes=[pltpu.VMEM(block, f32)] * 2
        + [pltpu.VMEM(block, bf16)] * 4
        + [
            pltpu.VMEM((2,) + block[1:], bf16),
            pltpu.VMEM((chips, part, width), bf16),
            pltpu.VMEM((chips, part, width), f32),
            pltpu.VMEM((chips - 1, part, width), bf16),
            pltpu.VMEM((tilts, third, width), f32),
            pltpu.VMEM((2 * third // 3, width), f32),
            pltpu.VMEM((tilts - 1, third, width), f32),
            pltpu.VMEM((2, chips, tilts, 2 * third // 3, width), f32),
        ]
        + [dma((3, 2)), dma((3, 2)), dma((4,)), dma((2,))]
        + [dma((1,))] * 2
        + [dma((chips - 1,))] * 2
        + [dma((tilts - 1,))] * 4
        + [dma((chips - 1,))] * 2
        + [dma((1,))] * 2,
        compiler_params=pltpu.CompilerParams(
            collective_id=2, has_side_effects=True, vmem_limit_bytes=20 * 1024 * 1024
        ),
    )(grads, sums)


def local(tilts, devices, intensity, positions, counts, object_field, probe):
    width = probe.shape[-1]
    rows = object_field.shape[2]
    reach = width // rows
    assert reach == 2 and devices % 2 == 0
    forward, inverse = dft_tables(width)
    band, frames, probe_v, forward, inverse, places = gather(
        devices, object_field, intensity, probe, forward, inverse, positions[0].T
    )
    parts = (2, devices // 2, 3 * width // devices, width)
    grads, sums = frame_sums(
        reach, tilts, parts, places, counts, frames, band, probe_v, forward, inverse
    )
    return tuple(exchange(tilts, devices, width, rows, grads, sums))


def solution(mesh):
    placed = (
        P("tilt", "pos", None, None),
        P("tilt", "pos", None),
        P("tilt", "pos"),
        P("tilt", None, "pos", None),
        P(),
    )
    return jax.shard_map(
        functools.partial(local, mesh.shape["tilt"], mesh.shape["pos"]),
        mesh=mesh,
        in_specs=placed,
        out_specs=(P("tilt", None, "pos", None), P()),
        check_vma=False,
    )
```

time: 81.4 us -> 71.1 us (0.87)
  Pallas kernels: 70.7 us -> 61.2 us
  local copies, waits for them, and re-layouts: 8.92 us -> 7.96 us
    pallas_call x1, Pallas kernels: 46 us -> 34.3 us  [exchange(): pl.pallas_call(functools.partial(exchange_kernel, tilts, devices), out_sh...]
    pallas_call x1, Pallas kernels: 13.2 us -> 16 us  [gather(): pl.pallas_call(functools.partial(gather_kernel, devices), out_shape=[jax....]
    unnamed x16 -> x14, local copies, waits for them, and re-layouts: 8.92 us -> 7.96 us
where the time goes in v1:
time: 71.1 us; the launch traced here: 70.5 us
  Pallas kernels  61.2 us (86%)
  local copies, waits for them, and re-layouts  7.96 us (11%)
  between operations  1.31 us (2%)
    pallas_call x1, Pallas kernels, exchange(): pl.pallas_call(functools.partial(exchange_kernel, tilts, devices), out_sh...  34.3 us
    pallas_call x1, Pallas kernels, gather(): pl.pallas_call(functools.partial(gather_kernel, devices), out_shape=[jax....  16 us
    pallas_call x1, Pallas kernels, frame_sums(): pl.pallas_call(functools.partial(frames_kernel, reach, tilts), out_shape=...  10.9 us
    unnamed x14, local copies, waits for them, and re-layouts  7.96 us

profile of v1, /device:TPU:0, one launch (start us, length us, event | category | flops | bytes accessed | tf_op | source)
XLA Modules:
  0.0 70.5 jit_solution(369806463256658113)
XLA Ops:
  1.3 0.0 copy-start
  1.3 1.6 %copy-done = bf16[1,16,256,256]{3,2,1,0:T(8,128)(2,1)S(1)} copy-done((bf16[1,16,256,256]{3,2,1,0:T(8,128)(2,1)S(1)}, bf16[1,16,256,256]{3,2,1,0:T(8,128)(2,1)}, u32[]{:S(2)}) %copy-start) | copy-done | bytes 2097176
  2.9 0.0 copy-start.1
  2.9 1.0 %copy-done.1 = f32[2,256,256]{2,1,0:T(8,128)S(1)} copy-done((f32[2,256,256]{2,1,0:T(8,128)S(1)}, f32[2,256,256]{2,1,0:T(8,128)}, u32[]{:S(2)}) %copy-start.1) | copy-done | bytes 524312
  3.9 0.0 copy-start.2
  3.9 1.0 %copy-done.2 = bf16[512,512]{1,0:T(8,128)(2,1)S(1)} copy-done((bf16[512,512]{1,0:T(8,128)(2,1)S(1)}, bf16[512,512]{1,0:T(8,128)(2,1)}, u32[]{:S(2)}) %copy-start.2) | copy-done | bytes 524312
  5.0 0.0 copy-start.3
  5.0 1.0 %copy-done.3 = bf16[512,512]{1,0:T(8,128)(2,1)S(1)} copy-done((bf16[512,512]{1,0:T(8,128)(2,1)S(1)}, bf16[512,512]{1,0:T(8,128)(2,1)}, u32[]{:S(2)}) %copy-start.3) | copy-done | bytes 524312
  6.0 0.0 copy-start.4
  6.0 1.0 %copy-done.4 = bf16[1,2,96,768]{3,2,1,0:T(8,128)(2,1)S(1)} copy-done((bf16[1,2,96,768]{3,2,1,0:T(8,128)(2,1)S(1)}, bf16[1,2,96,768]{3,2,1,0:T(8,128)(2,1)}, u32[]{:S(2)}) %copy-start.4) | copy-done | bytes 294936
  7.0 0.0 copy-start.5
  7.0 0.7 copy-done.5
  7.6 16.0 %shard_map.86 = (f32[2,7,480,128]{3,2,1,0:T(8,128)S(1)}, bf16[16,256,256]{2,1,0:T(8,128)(2,1)S(1)}, f32[2,256,256]{2,1,0:T(8,128)S(1)}, bf16[512,512]{1,0:T(8,12...) custom-call(bf16[1,2,96,768]{3,2,1,0:T(8,128)(2,1)S(1)} %copy-done.4, ...), custom_call_target="tpu_custom_call" | custom-call | tf_op jit(solution)/shard_map/pallas_call | solution.py:373
  23.7 10.9 %shard_map.87 = (f32[2,7,480,128]{3,2,1,0:T(8,128)S(1)}, f32[2,4,96,256]{3,2,1,0:T(8,128)S(1)}) custom-call(s32[2,16]{1,0:T(2,128)S(1)} %get-tuple-element.10.pos_any, s32[1,1]{1,0:T(1,128)S(6)} %copy.11.count_ref, bf16[16,256,256]{2,1,0:T(8,128)(2,1)S(1)} %get-tuple-element.11.frames_ref, f32[2,7,480,128]{3,2,1,0:T(8,128)S(1)} %get-tuple-element.12.band, ...), custom_call_target="tpu_custom_call" | custom-call | tf_op jit(solution)/shard_map/pallas_call | solution.py:160
  34.5 34.3 %shard_map.88 = (f32[1,2,96,768]{3,2,1,0:T(8,128)S(1)}, f32[2,256,256]{2,1,0:T(8,128)S(1)}) custom-call(f32[2,7,480,128]{3,2,1,0:T(8,128)S(1)} %get-tuple-element.16.refs_0_, f32[2,4,96,256]{3,2,1,0:T(8,128)S(1)} %get-tuple-element.17.refs_1_), custom_call_target="tpu_custom_call" | custom-call | tf_op jit(solution)/shard_map/pallas_call | solution.py:609
  68.8 0.8 %copy.12 = f32[1,2,96,768]{3,2,1,0:T(8,128)} copy(f32[1,2,96,768]{3,2,1,0:T(8,128)S(1)} %get-tuple-element.20) | data formatting | bytes 1179648
  69.7 0.8 %copy.13 = f32[2,256,256]{2,1,0:T(8,128)} copy(f32[2,256,256]{2,1,0:T(8,128)S(1)} %get-tuple-element.21) | data formatting | bytes 1048576
Async XLA Ops:
  1.3 1.6 %copy-start = (bf16[1,16,256,256]{3,2,1,0:T(8,128)(2,1)S(1)}, bf16[1,16,256,256]{3,2,1,0:T(8,128)(2,1)}, u32[]{:S(2)}) copy-start(bf16[1,16,256,256]{3,2,1,0:T(8,128)(2,1)} %frames_any.1) | copy-start | bytes 6291460
  2.9 1.0 %copy-start.1 = (f32[2,256,256]{2,1,0:T(8,128)S(1)}, f32[2,256,256]{2,1,0:T(8,128)}, u32[]{:S(2)}) copy-start(f32[2,256,256]{2,1,0:T(8,128)} %probe_any.1) | copy-start | bytes 1572868
  3.9 1.0 %copy-start.2 = (bf16[512,512]{1,0:T(8,128)(2,1)S(1)}, bf16[512,512]{1,0:T(8,128)(2,1)}, u32[]{:S(2)}) copy-start(bf16[512,512]{1,0:T(8,128)(2,1)} %constant.11.inv_any) | copy-start | bytes 1572868
  5.0 1.0 %copy-start.3 = (bf16[512,512]{1,0:T(8,128)(2,1)S(1)}, bf16[512,512]{1,0:T(8,128)(2,1)}, u32[]{:S(2)}) copy-start(bf16[512,512]{1,0:T(8,128)(2,1)} %constant.10.fwd_any) | copy-start | bytes 1572868
  6.0 1.0 %copy-start.4 = (bf16[1,2,96,768]{3,2,1,0:T(8,128)(2,1)S(1)}, bf16[1,2,96,768]{3,2,1,0:T(8,128)(2,1)}, u32[]{:S(2)}) copy-start(bf16[1,2,96,768]{3,2,1,0:T(8,128)(2,1)} %field_any.1) | copy-start | bytes 884740
  7.0 0.7 copy-start.5

commit v2 on v1

--- a/solution.py
+++ b/solution.py
@@ -370,15 +370,18 @@
     block = (planes, rows, columns)
     groups = columns // LANES
     dma = pltpu.SemaphoreType.DMA
+    held = 4 * planes * (groups + 1) * 5 * rows * LANES + sum(
+        a.size * a.dtype.itemsize for a in (frames, probe, forward, inverse)
+    )
     return pl.pallas_call(
         functools.partial(gather_kernel, devices),
         out_shape=[
-            jax.ShapeDtypeStruct((planes, groups + 1, 5 * rows, LANES), jnp.float32),
-            jax.ShapeDtypeStruct(frames.shape[1:], frames.dtype),
-            jax.ShapeDtypeStruct(probe.shape, probe.dtype),
-            jax.ShapeDtypeStruct(forward.shape, forward.dtype),
-            jax.ShapeDtypeStruct(inverse.shape, inverse.dtype),
-            jax.ShapeDtypeStruct(positions.shape, positions.dtype),
+            pltpu.VMEM((planes, groups + 1, 5 * rows, LANES), jnp.float32),
+            pltpu.VMEM(frames.shape[1:], frames.dtype),
+            pltpu.VMEM(probe.shape, probe.dtype),
+            pltpu.VMEM(forward.shape, forward.dtype),
+            pltpu.VMEM(inverse.shape, inverse.dtype),
+            pltpu.VMEM(positions.shape, positions.dtype),
         ],
         in_specs=[hbm] * 6,
         out_specs=[vmem] * 6,
@@ -393,7 +396,7 @@
             dma((6,)),
         ],
         compiler_params=pltpu.CompilerParams(
-            collective_id=1, has_side_effects=True, vmem_limit_bytes=16 * 1024 * 1024
+            collective_id=1, has_side_effects=True, vmem_limit_bytes=62 * 1024 * 1024 - held
         ),
     )(field, frames, probe, forward, inverse, positions)
 

time: 71.1 us -> 63.7 us (0.90); the launches traced: 70.5 us -> 63.9 us
  local copies, waits for them, and re-layouts: 7.96 us -> 1.61 us
    unnamed x14 -> x2, local copies, waits for them, and re-layouts: 7.96 us -> 1.61 us
where the time goes in v2:
time: 63.7 us; the launch traced here: 63.9 us
  Pallas kernels  60.9 us (96%)
  local copies, waits for them, and re-layouts  1.61 us (3%)
  between operations  1.3 us (2%)
    pallas_call x1, Pallas kernels, exchange(): pl.pallas_call(functools.partial(exchange_kernel, tilts, devices), out_sh...  34.4 us
    pallas_call x1, Pallas kernels, gather(): pl.pallas_call(functools.partial(gather_kernel, devices), out_shape=[pltp...  16 us
    pallas_call x1, Pallas kernels, frame_sums(): pl.pallas_call(functools.partial(frames_kernel, reach, tilts), out_shape=...  10.6 us
    unnamed x2, local copies, waits for them, and re-layouts  1.61 us

profile of v2, /device:TPU:0, one launch (start us, length us, event | category | flops | bytes accessed | tf_op | source)
XLA Modules:
  0.0 63.9 jit_solution(15437516389214889064)
XLA Ops:
  1.3 16.0 %shard_map.86 = (f32[2,7,480,128]{3,2,1,0:T(8,128)S(1)}, bf16[16,256,256]{2,1,0:T(8,128)(2,1)S(1)}, f32[2,256,256]{2,1,0:T(8,128)S(1)}, bf16[512,512]{1,0:T(8,12...) custom-call(bf16[1,2,96,768]{3,2,1,0:T(8,128)(2,1)} %field_any.1, bf16[1,16,256,256]{3,2,1,0:T(8,128)(2,1)} %frames_any.1, ...), custom_call_target="tpu_custom_call" | custom-call | tf_op jit(solution)/shard_map/pallas_call | solution.py:376
  17.3 10.6 %shard_map.87 = (f32[2,7,480,128]{3,2,1,0:T(8,128)S(1)}, f32[2,4,96,256]{3,2,1,0:T(8,128)S(1)}) custom-call(s32[2,16]{1,0:T(2,128)S(1)} %get-tuple-element.10.pos_any, s32[1,1]{1,0:T(1,128)S(6)} %copy.11.count_ref, bf16[16,256,256]{2,1,0:T(8,128)(2,1)S(1)} %get-tuple-element.11.frames_ref, f32[2,7,480,128]{3,2,1,0:T(8,128)S(1)} %get-tuple-element.12.band, ...), custom_call_target="tpu_custom_call" | custom-call | tf_op jit(solution)/shard_map/pallas_call | solution.py:160
  27.8 34.4 %shard_map.88 = (f32[1,2,96,768]{3,2,1,0:T(8,128)S(1)}, f32[2,256,256]{2,1,0:T(8,128)S(1)}) custom-call(f32[2,7,480,128]{3,2,1,0:T(8,128)S(1)} %get-tuple-element.16.refs_0_, f32[2,4,96,256]{3,2,1,0:T(8,128)S(1)} %get-tuple-element.17.refs_1_), custom_call_target="tpu_custom_call" | custom-call | tf_op jit(solution)/shard_map/pallas_call | solution.py:612
  62.2 0.8 %copy.12 = f32[1,2,96,768]{3,2,1,0:T(8,128)} copy(f32[1,2,96,768]{3,2,1,0:T(8,128)S(1)} %get-tuple-element.20) | data formatting | bytes 1179648
  63.1 0.8 %copy.13 = f32[2,256,256]{2,1,0:T(8,128)} copy(f32[2,256,256]{2,1,0:T(8,128)S(1)} %get-tuple-element.21) | data formatting | bytes 1048576

commit v3 on v2

--- a/solution.py
+++ b/solution.py
@@ -1,7 +1,9 @@
 import functools
+import math
 
 import jax
 import jax.numpy as jnp
+import ml_dtypes
 import numpy as np
 from jax import lax
 from jax.experimental import pallas as pl
@@ -9,6 +11,21 @@
 from jax.sharding import PartitionSpec as P
 
 LANES = 128
+GROUP = 4
+EXTRACT = 256
+SPREAD = 64
+
+
+def orders(length):
+    quarter, halfway = length // 4, length // 2
+    low = np.concatenate([2 * np.arange(quarter), 2 * np.arange(quarter) + 1])
+    mirror = (length - low) % length
+    mirror[0] = halfway
+    split = np.concatenate([low, mirror])
+    plain = np.arange(halfway)
+    mirror = (length - plain) % length
+    mirror[0] = halfway
+    return split, np.concatenate([plain, mirror])
 
 
 def dft_tables(length):
@@ -18,12 +35,33 @@
     )
     cosine = np.cos(phase) / np.sqrt(length)
     sine = np.sin(phase) / np.sqrt(length)
-    forward = np.block([[cosine, -sine], [sine, cosine]])
-    inverse = np.block([[cosine, sine], [-sine, cosine]])
-    return (
-        jnp.asarray(forward.astype(np.float32)).astype(jnp.bfloat16),
-        jnp.asarray(inverse.astype(np.float32)).astype(jnp.bfloat16),
-    )
+    halfway = length // 2
+    rows, columns = orders(length)
+
+    def paired(order):
+        table = np.concatenate([cosine[:, order[:halfway]], sine[:, order[:halfway]]], 1)
+        table[:, halfway] = cosine[:, halfway]
+        return table
+
+    forward_columns = paired(columns)
+    forward_rows = paired(rows).T
+    quarter = length // 4
+    even = np.concatenate([rows[:quarter], rows[halfway : halfway + quarter]])
+    odd = np.concatenate([rows[quarter:halfway], rows[halfway + quarter :]])
+
+    def side(ks):
+        c, s = cosine[:halfway, ks], sine[:halfway, ks]
+        return np.block([[c, -s], [s, c]])
+
+    inverse_rows = np.concatenate([side(even), side(odd)], 0)
+    c, s = cosine[columns], sine[columns]
+    inverse_columns = np.block([[c, s], [-s, c]])
+    stack = np.concatenate([forward_columns, forward_rows, inverse_rows], 0)
+
+    def cast(table):
+        return jnp.asarray(table.astype(np.float32)).astype(jnp.bfloat16)
+
+    return cast(stack), cast(inverse_columns)
 
 
 def frames_kernel(
@@ -39,6 +77,7 @@
     total,
     chunks_ref,
     sums_ref,
+    patch_ref,
     pos_ref,
     pos_sem,
 ):
@@ -53,94 +92,153 @@
     first = (lax.axis_index("pos") - reach) * rows
     fetch.wait()
 
-    lane = lax.broadcasted_iota(jnp.int32, (width, LANES), 1)
+    lane = lax.broadcasted_iota(jnp.int32, (EXTRACT, LANES), 1)
+    wide_lane = lax.broadcasted_iota(jnp.int32, (SPREAD, LANES), 1)
+    edge = lane == 0
+    top = lax.broadcasted_iota(jnp.int32, (8, width), 0) == 0
+    mid = width // 2
+
+    def dot(a, b):
+        return jnp.dot(a, b, preferred_element_type=jnp.float32)
 
     def some_frames(at):
-        pr, pi = probe_ref[0], probe_ref[1]
-        spots, patches, exits = [], [], []
+        spots = []
         for i in at:
-            r = pos_ref[0, i] - first
             q = pos_ref[1, i]
-            qb, qs = q // LANES, lax.rem(q, LANES)
-            spots.append((r, qb, qs))
-            near = lane < LANES - qs
-            back_shift = lax.rem(LANES - qs, LANES)
-            patch = []
-            for c in range(2):
-                rolled = [
-                    pltpu.roll(band[c, qb + j, pl.ds(r, width), :], back_shift, 1)
-                    for j in range(wide + 1)
-                ]
-                patch.append(
+            spots.append((pos_ref[0, i] - first, q // LANES, lax.rem(q, LANES)))
+        pieces = [[] for _ in at]
+        for start in range(0, width, EXTRACT):
+            pr, pi = probe_ref[0, start : start + EXTRACT], probe_ref[1, start : start + EXTRACT]
+            exits = []
+            for n, (r, qb, qs) in enumerate(spots):
+                near = lane < LANES - qs
+                back_shift = lax.rem(LANES - qs, LANES)
+                patch = []
+                for c in range(2):
+                    rolled = [
+                        pltpu.roll(band[c, qb + j, pl.ds(r + start, EXTRACT), :], back_shift, 1)
+                        for j in range(wide + 1)
+                    ]
+                    patch.append(
+                        jnp.concatenate(
+                            [jnp.where(near, rolled[j], rolled[j + 1]) for j in range(wide)], 1
+                        )
+                    )
+                    patch_ref[n, c, start : start + EXTRACT] = patch[c]
+                xr, xi = patch
+                exits.append((pr * xr - pi * xi).astype(jnp.bfloat16))
+                exits.append((pr * xi + pi * xr).astype(jnp.bfloat16))
+            out = dot(jnp.concatenate(exits, 0), fwd_ref[0:width])
+            for n in range(len(at)):
+                re = out[2 * n * EXTRACT : (2 * n + 1) * EXTRACT]
+                im = out[(2 * n + 1) * EXTRACT : (2 * n + 2) * EXTRACT]
+                u, v, uu, vv = re[:, :LANES], re[:, LANES:], im[:, :LANES], im[:, LANES:]
+                pieces[n].append(
                     jnp.concatenate(
-                        [jnp.where(near, rolled[j], rolled[j + 1]) for j in range(wide)], 1
-                    )
+                        [
+                            u + jnp.where(edge, 0.0, vv),
+                            jnp.where(edge, v, u - vv),
+                            uu - jnp.where(edge, 0.0, v),
+                            jnp.where(edge, vv, uu + v),
+                        ],
+                        1,
+                    ).astype(jnp.bfloat16)
                 )
-            xr, xi = patch
-            patches.append((xr, xi))
-            exits.append(
+        backs = []
+        for n, i in enumerate(at):
+            far = dot(fwd_ref[width : 2 * width], jnp.concatenate(pieces[n], 0))
+            u, v = far[:mid, :width], far[mid:, :width]
+            uu, vv = far[:mid, width:], far[mid:, width:]
+            fr = jnp.concatenate(
+                [
+                    u[:8] + jnp.where(top, 0.0, vv[:8]),
+                    u[8:] + vv[8:],
+                    jnp.where(top, v[:8], u[:8] - vv[:8]),
+                    u[8:] - vv[8:],
+                ],
+                0,
+            )
+            fi = jnp.concatenate(
+                [
+                    uu[:8] - jnp.where(top, 0.0, v[:8]),
+                    uu[8:] - v[8:],
+                    jnp.where(top, vv[:8], uu[:8] + v[:8]),
+                    uu[8:] + v[8:],
+                ],
+                0,
+            )
+            misfit = fr * fr + fi * fi - frames_ref[i].astype(jnp.float32)
+            br = (fr * misfit).astype(jnp.bfloat16)
+            bi = (fi * misfit).astype(jnp.bfloat16)
+            q = mid // 2
+            backs.append(
+                (
+                    jnp.concatenate([br[:q], br[mid : mid + q], bi[:q], bi[mid : mid + q]], 0),
+                    jnp.concatenate([br[q:mid], br[mid + q :], bi[q:mid], bi[mid + q :]], 0),
+                )
+            )
+        mids = []
+        for n, i in enumerate(at):
+            ev = dot(fwd_ref[2 * width : 3 * width], backs[n][0])
+            od = dot(fwd_ref[3 * width :], backs[n][1])
+            add, sub = (ev + od).astype(jnp.bfloat16), (ev - od).astype(jnp.bfloat16)
+            mids.append(
                 jnp.concatenate(
                     [
-                        (pr * xr - pi * xi).astype(jnp.bfloat16),
-                        (pr * xi + pi * xr).astype(jnp.bfloat16),
+                        jnp.concatenate([add[:mid], sub[:mid]], 0),
+                        jnp.concatenate([add[mid:], sub[mid:]], 0),
                     ],
                     1,
                 )
             )
-        halves = jnp.dot(
-            jnp.concatenate(exits, 0), fwd_ref[...], preferred_element_type=jnp.float32
-        ).astype(jnp.bfloat16)
-        mids = []
-        for n, i in enumerate(at):
-            half = halves[n * width : (n + 1) * width]
-            half = jnp.concatenate([half[:, :width], half[:, width:]], 0)
-            far = jnp.dot(inv_ref[...], half, preferred_element_type=jnp.float32)
-            fr, fi = far[:width], far[width:]
-            misfit = fr * fr + fi * fi - frames_ref[i].astype(jnp.float32)
-            back = jnp.concatenate(
-                [(fr * misfit).astype(jnp.bfloat16), (fi * misfit).astype(jnp.bfloat16)], 0
-            )
-            mid = jnp.dot(fwd_ref[...], back, preferred_element_type=jnp.float32).astype(
-                jnp.bfloat16
-            )
-            mids.append(jnp.concatenate([mid[:width], mid[width:]], 1))
-        waves = jnp.dot(
-            jnp.concatenate(mids, 0), inv_ref[...], preferred_element_type=jnp.float32
-        )
-        sums = [0.0, 0.0, 0.0]
-        for n, i in enumerate(at):
-            xr, xi = patches[n]
-            wave = waves[n * width : (n + 1) * width]
-            wr, wi = wave[:, :width], wave[:, width:]
-            sums[0] += xr * wr + xi * wi
-            sums[1] += xr * wi - xi * wr
-            sums[2] += xr * xr + xi * xi
-            r, qb, qs = spots[n]
-            far_side = lane >= qs
-            for c in range(2):
-                grad = pr * wr + pi * wi if c == 0 else pr * wi - pi * wr
-                grad = grad.astype(jnp.bfloat16).astype(jnp.float32)
-                rolled = [
-                    pltpu.roll(grad[:, j * LANES : (j + 1) * LANES], qs, 1)
-                    for j in range(wide)
-                ]
-                zero = jnp.zeros_like(rolled[0])
-                for j in range(wide + 1):
-                    here = rolled[j] if j < wide else zero
-                    before = rolled[j - 1] if j > 0 else zero
-                    total[c, qb + j, pl.ds(r, width), :] += jnp.where(far_side, here, before)
-        for k in range(3):
-            sums_ref[k] += sums[k]
+        for start in range(0, width, SPREAD):
+            waves = dot(
+                jnp.concatenate([m[start : start + SPREAD] for m in mids], 0), inv_ref[...]
+            )
+            pr, pi = probe_ref[0, start : start + SPREAD], probe_ref[1, start : start + SPREAD]
+            sums = [0.0, 0.0, 0.0]
+            for n, (r, qb, qs) in enumerate(spots):
+                xr = patch_ref[n, 0, start : start + SPREAD]
+                xi = patch_ref[n, 1, start : start + SPREAD]
+                wave = waves[n * SPREAD : (n + 1) * SPREAD]
+                wr, wi = wave[:, :width], wave[:, width:]
+                sums[0] += xr * wr + xi * wi
+                sums[1] += xr * wi - xi * wr
+                sums[2] += xr * xr + xi * xi
+                far_side = wide_lane >= qs
+                for c in range(2):
+                    grad = pr * wr + pi * wi if c == 0 else pr * wi - pi * wr
+                    grad = grad.astype(jnp.bfloat16).astype(jnp.float32)
+                    rolled = [
+                        pltpu.roll(grad[:, j * LANES : (j + 1) * LANES], qs, 1)
+                        for j in range(wide)
+                    ]
+                    zero = jnp.zeros_like(rolled[0])
+                    for j in range(wide + 1):
+                        here = rolled[j] if j < wide else zero
+                        before = rolled[j - 1] if j > 0 else zero
+                        total[c, qb + j, pl.ds(r + start, SPREAD), :] += jnp.where(
+                            far_side, here, before
+                        )
+            for k in range(3):
+                sums_ref[k, start : start + SPREAD] += sums[k]
 
     count = count_ref[0, 0]
-
-    @pl.loop(0, count // 2)
+    group = GROUP
+
+    @pl.loop(0, count // group)
     def _(i):
-        some_frames([2 * i, 2 * i + 1])
-
-    @pl.when(lax.rem(count, 2) == 1)
-    def _():
-        some_frames([count - 1])
+        some_frames([group * i + n for n in range(group)])
+
+    done = count // group * group
+    for size in (2, 1):
+        left = (count - done) // size
+
+        @pl.when(left > 0)
+        def _(done=done, size=size):
+            some_frames([done + n for n in range(size)])
+
+        done = done + left * size
 
     pairs, chips, _, _ = chunks_ref.shape
     chunk = chunks_ref.shape[2] // (3 * tilts)
@@ -167,6 +265,7 @@
         out_specs=[vmem] * 2,
         scratch_shapes=[
             pltpu.VMEM((3,) + probe.shape[1:], jnp.float32),
+            pltpu.VMEM((GROUP, 2) + probe.shape[1:], jnp.float32),
             pltpu.SMEM(positions.shape, jnp.int32),
             pltpu.SemaphoreType.DMA,
         ],
@@ -217,6 +316,7 @@
     fwd_any,
     inv_any,
     pos_any,
+    moves_any,
     band,
     frames_ref,
     probe_ref,
@@ -226,6 +326,8 @@
     own,
     slots,
     stage,
+    raw_ref,
+    moves_ref,
     out_sem,
     in_sem,
     relay_out,
@@ -247,7 +349,8 @@
                 (probe_any, probe_ref),
                 (fwd_any, fwd_ref),
                 (inv_any, inv_ref),
-                (frames_any.at[0], frames_ref),
+                (moves_any, moves_ref),
+                (frames_any.at[0], raw_ref),
             ]
         )
     ]
@@ -260,6 +363,24 @@
                 band[c, g, pl.ds(b * rows, rows), :] = src[
                     c, :, g * LANES : (g + 1) * LANES
                 ].astype(jnp.float32)
+
+    def reorder():
+        slots_of, width = raw_ref.shape[0], raw_ref.shape[1]
+        some = math.gcd(slots_of, 4)
+
+        @pl.loop(0, slots_of // some)
+        def _(i):
+            moved = jnp.dot(
+                jnp.concatenate([raw_ref[i * some + n] for n in range(some)], 0),
+                moves_ref[1],
+                preferred_element_type=jnp.float32,
+            ).astype(jnp.bfloat16)
+            for n in range(some):
+                frames_ref[i * some + n] = jnp.dot(
+                    moves_ref[0],
+                    moved[n * width : (n + 1) * width],
+                    preferred_element_type=jnp.float32,
+                ).astype(frames_ref.dtype)
 
     def role(odd):
         partner = p - 1 if odd else p + 1
@@ -326,6 +447,10 @@
                 to_stage.wait_recv()
                 staged_right.start()
 
+        for load in loads:
+            load.wait()
+        reorder()
+
         @pl.when(outer)
         def _():
             for c in range(2):
@@ -342,8 +467,6 @@
                 arrived(opposite, c)
             place(slots.at[opposite], opposite)
 
-        for load in loads:
-            load.wait()
         pl.when(has_left)(to_left[0].wait_send)
         pl.when(has_right)(to_right[0].wait_send)
         if relayed(devices):
@@ -363,7 +486,7 @@
     pl.when(lax.rem(p, 2) == 1)(lambda: role(True))
 
 
-def gather(devices, field, frames, probe, forward, inverse, positions):
+def gather(devices, field, frames, probe, forward, inverse, positions, moves):
     hbm = pl.BlockSpec(memory_space=pltpu.HBM)
     vmem = pl.BlockSpec(memory_space=pltpu.VMEM)
     _, planes, rows, columns = field.shape
@@ -383,22 +506,24 @@
             pltpu.VMEM(inverse.shape, inverse.dtype),
             pltpu.VMEM(positions.shape, positions.dtype),
         ],
-        in_specs=[hbm] * 6,
+        in_specs=[hbm] * 7,
         out_specs=[vmem] * 6,
         scratch_shapes=[
             pltpu.VMEM(block, field.dtype),
             pltpu.VMEM((5,) + block, field.dtype),
             pltpu.VMEM((rows, columns), field.dtype),
+            pltpu.VMEM(frames.shape[1:], frames.dtype),
+            pltpu.VMEM(moves.shape, moves.dtype),
             dma((4, 2)),
             dma((5, 2)),
             dma((3,)),
             dma((1,)),
-            dma((6,)),
+            dma((7,)),
         ],
         compiler_params=pltpu.CompilerParams(
             collective_id=1, has_side_effects=True, vmem_limit_bytes=62 * 1024 * 1024 - held
         ),
-    )(field, frames, probe, forward, inverse, positions)
+    )(field, frames, probe, forward, inverse, positions, moves)
 
 
 def exchange_kernel(tilts, devices, *refs):
@@ -647,8 +772,13 @@
     reach = width // rows
     assert reach == 2 and devices % 2 == 0
     forward, inverse = dft_tables(width)
+    row_order, column_order = orders(width)
+    identity = np.eye(width, dtype=np.float32)
+    moves = jnp.asarray(
+        np.stack([identity[row_order], identity[column_order].T]).astype(ml_dtypes.bfloat16)
+    )
     band, frames, probe_v, forward, inverse, places = gather(
-        devices, object_field, intensity, probe, forward, inverse, positions[0].T
+        devices, object_field, intensity, probe, forward, inverse, positions[0].T, moves
     )
     parts = (2, devices // 2, 3 * width // devices, width)
     grads, sums = frame_sums(

time: 63.7 us -> 56.4 us (0.89)
  Pallas kernels: 60.9 us -> 53.6 us
    pallas_call x1, Pallas kernels: 10.6 us -> 6.66 us  [frame_sums(): pl.pallas_call(functools.partial(frames_kernel, reach, tilts), out_shape=...]
    pallas_call x1, Pallas kernels: 34.4 us -> 30.9 us  [exchange(): pl.pallas_call(functools.partial(exchange_kernel, tilts, devices), out_sh...]
where the time goes in v3:
time: 56.4 us; the launch traced here: 56.5 us
  Pallas kernels  53.6 us (95%)
  local copies, waits for them, and re-layouts  1.61 us (3%)
  between operations  1.3 us (2%)
    pallas_call x1, Pallas kernels, exchange(): pl.pallas_call(functools.partial(exchange_kernel, tilts, devices), out_sh...  30.9 us
    pallas_call x1, Pallas kernels, gather(): pl.pallas_call(functools.partial(gather_kernel, devices), out_shape=[pltp...  16 us
    pallas_call x1, Pallas kernels, frame_sums(): pl.pallas_call(functools.partial(frames_kernel, reach, tilts), out_shape=...  6.66 us
    unnamed x2, local copies, waits for them, and re-layouts  1.61 us

profile of v3, /device:TPU:0, one launch (start us, length us, event | category | flops | bytes accessed | tf_op | source)
XLA Modules:
  0.0 56.5 jit_solution(5295811463106021334)
XLA Ops:
  1.3 16.0 %shard_map.95 = (f32[2,7,480,128]{3,2,1,0:T(8,128)S(1)}, bf16[16,256,256]{2,1,0:T(8,128)(2,1)S(1)}, f32[2,256,256]{2,1,0:T(8,128)S(1)}, bf16[1024,256]{1,0:T(8,1...) custom-call(bf16[1,2,96,768]{3,2,1,0:T(8,128)(2,1)} %field_any.1, bf16[1,16,256,256]{3,2,1,0:T(8,128)(2,1)} %frames_any.1, ...), custom_call_target="tpu_custom_call" | custom-call | tf_op jit(solution)/shard_map/pallas_call | solution.py:499
  17.3 6.7 %shard_map.96 = (f32[2,7,480,128]{3,2,1,0:T(8,128)S(1)}, f32[2,4,96,256]{3,2,1,0:T(8,128)S(1)}) custom-call(s32[2,16]{1,0:T(2,128)S(1)} %get-tuple-element.10.pos_any, s32[1,1]{1,0:T(1,128)S(6)} %copy.12.count_ref, bf16[16,256,256]{2,1,0:T(8,128)(2,1)S(1)} %get-tuple-element.11.frames_ref, f32[2,7,480,128]{3,2,1,0:T(8,128)S(1)} %get-tuple-element.12.band, ...), custom_call_target="tpu_custom_call" | custom-call | tf_op jit(solution)/shard_map/pallas_call | solution.py:258
  23.9 30.9 %shard_map.97 = (f32[1,2,96,768]{3,2,1,0:T(8,128)S(1)}, f32[2,256,256]{2,1,0:T(8,128)S(1)}) custom-call(f32[2,7,480,128]{3,2,1,0:T(8,128)S(1)} %get-tuple-element.16.refs_0_, f32[2,4,96,256]{3,2,1,0:T(8,128)S(1)} %get-tuple-element.17.refs_1_), custom_call_target="tpu_custom_call" | custom-call | tf_op jit(solution)/shard_map/pallas_call | solution.py:737
  54.9 0.8 %copy.13 = f32[1,2,96,768]{3,2,1,0:T(8,128)} copy(f32[1,2,96,768]{3,2,1,0:T(8,128)S(1)} %get-tuple-element.20) | data formatting | bytes 1179648
  55.7 0.8 %copy.14 = f32[2,256,256]{2,1,0:T(8,128)} copy(f32[2,256,256]{2,1,0:T(8,128)S(1)} %get-tuple-element.21) | data formatting | bytes 1048576

commit v4 on v3

--- a/solution.py
+++ b/solution.py
@@ -406,25 +406,36 @@
         def arrived(slot, c):
             copy(own, slot, c, 0, partner).wait_recv()
 
+        to_near, to_far = (to_right, to_left) if odd else (to_left, to_right)
+        has_near, has_far = (has_right, has_left) if odd else (has_left, has_right)
         if relayed(devices):
             across = lax.rem(p + 4, 8)
-            to_stage = send(own.at[1], stage, relay_out.at[0], relay_in.at[0], t, across)
-            staged_right = send(
-                stage, slots.at[slot_right, 1], relay_out.at[1], in_sem.at[slot_right, 1], t, 4
-            )
-            staged_left = send(
-                stage, slots.at[slot_left, 1], relay_out.at[2], in_sem.at[slot_left, 1], t, 3
-            )
-            middle = (chip == 1) | (chip == 2)
-            pl.when(middle)(to_stage.start)
-            pl.when(has_left)(to_left[0].start)
-            pl.when(has_right)(to_right[0].start)
-            pl.when(has_left & (chip != 2))(to_left[1].start)
-            pl.when(has_right & (chip != 1))(to_right[1].start)
+            source, relay = (chip == 2, chip == 0) if odd else (chip == 1, chip == 3)
+            slot_far, pos_far = (slot_left, 3) if odd else (slot_right, 4)
+            direct = has_far & ~source
+            to_stage = [
+                send(own.at[c], stage.at[c], relay_out.at[0, c], relay_in.at[c], t, across)
+                for c in range(2)
+            ]
+            staged = [
+                send(
+                    stage.at[c],
+                    slots.at[slot_far, c],
+                    relay_out.at[1, c],
+                    in_sem.at[slot_far, c],
+                    t,
+                    pos_far,
+                )
+                for c in range(2)
+            ]
         else:
-            for c in range(2):
-                pl.when(has_left)(to_left[c].start)
-                pl.when(has_right)(to_right[c].start)
+            direct = has_far
+        for c in range(2):
+            if relayed(devices):
+                pl.when(source)(to_stage[c].start)
+            pl.when(has_near)(to_near[c].start)
+        for c in range(2):
+            pl.when(direct)(to_far[c].start)
         for c in range(2):
             to_partner[c].start()
         for load in loads:
@@ -435,21 +446,16 @@
         for c in range(2):
             arrived(from_partner, c)
         place(slots.at[from_partner], from_partner)
-        if relayed(devices):
-
-            @pl.when(chip == 0)
-            def _():
-                to_stage.wait_recv()
-                staged_left.start()
-
-            @pl.when(chip == 3)
-            def _():
-                to_stage.wait_recv()
-                staged_right.start()
-
         for load in loads:
             load.wait()
         reorder()
+        if relayed(devices):
+
+            @pl.when(relay)
+            def _():
+                for c in range(2):
+                    to_stage[c].wait_recv()
+                    staged[c].start()
 
         @pl.when(outer)
         def _():
@@ -467,17 +473,12 @@
                 arrived(opposite, c)
             place(slots.at[opposite], opposite)
 
-        pl.when(has_left)(to_left[0].wait_send)
-        pl.when(has_right)(to_right[0].wait_send)
-        if relayed(devices):
-            pl.when(middle)(to_stage.wait_send)
-            pl.when(has_left & (chip != 2))(to_left[1].wait_send)
-            pl.when(has_right & (chip != 1))(to_right[1].wait_send)
-            pl.when(chip == 0)(staged_left.wait_send)
-            pl.when(chip == 3)(staged_right.wait_send)
-        else:
-            pl.when(has_left)(to_left[1].wait_send)
-            pl.when(has_right)(to_right[1].wait_send)
+        for c in range(2):
+            pl.when(has_near)(to_near[c].wait_send)
+            pl.when(direct)(to_far[c].wait_send)
+            if relayed(devices):
+                pl.when(source)(to_stage[c].wait_send)
+                pl.when(relay)(staged[c].wait_send)
         for c in range(2):
             to_partner[c].wait_send()
             pl.when(outer)(forward[c].wait_send)
@@ -511,13 +512,13 @@
         scratch_shapes=[
             pltpu.VMEM(block, field.dtype),
             pltpu.VMEM((5,) + block, field.dtype),
-            pltpu.VMEM((rows, columns), field.dtype),
+            pltpu.VMEM(block, field.dtype),
             pltpu.VMEM(frames.shape[1:], frames.dtype),
             pltpu.VMEM(moves.shape, moves.dtype),
             dma((4, 2)),
             dma((5, 2)),
-            dma((3,)),
-            dma((1,)),
+            dma((2, 2)),
+            dma((2,)),
             dma((7,)),
         ],
         compiler_params=pltpu.CompilerParams(
@@ -527,11 +528,11 @@
 
 
 def exchange_kernel(tilts, devices, *refs):
-    grads, sums, object_ref, probe_ref = refs[:4]
-    mine, extra, from_left, from_right, near, distant, stage = refs[4:11]
-    half, got0, got1, plane, column, got2, result = refs[11:18]
-    obj_out, obj_in, stage_out, stage_in = refs[18:22]
-    out0, in0, out1, in1, out2, in2, out3, in3, out4, in4, out5, in5 = refs[22:]
+    grads, sums, mine, from_left, from_right, result = refs[:6]
+    extra, near, distant, stage = refs[6:10]
+    half, got0, got1, plane, column, got2 = refs[10:16]
+    obj_out, obj_in, stage_out, stage_in = refs[16:20]
+    out0, in0, out1, in1, out2, in2, out3, in3, out4, in4, out5, in5 = refs[20:]
     t, p = lax.axis_index("tilt"), lax.axis_index("pos")
     chip, chips = p // 2, devices // 2
     e = lax.rem(p, 2)
@@ -544,7 +545,20 @@
     def block(b):
         return grads.at[:, pl.ds(0, groups), pl.ds(b * rows, rows), :]
 
-    swap = send(sums.at[1 - e], got0, out0.at[0], in0.at[0], t, partner)
+    chips_rows = half.shape[1]
+    pieces = out0.shape[0]
+    piece = chips_rows // pieces
+    per = tilts // pieces
+
+    def cut(n):
+        return pl.ds(n * piece, piece)
+
+    swap = [
+        send(
+            sums.at[1 - e, :, cut(n), :], got0.at[:, cut(n), :], out0.at[n], in0.at[n], t, partner
+        )
+        for n in range(pieces)
+    ]
 
     def objects(odd, step):
         has = chip < chips - 1 if odd else chip > 0
@@ -631,35 +645,45 @@
         pl.when(e == 0)(lambda: objects(False, step))
         pl.when(e == 1)(lambda: objects(True, step))
 
-    swap.start()
+    for copy in swap:
+        copy.start()
     both(0)
-    swap.wait_recv()
-    half[...] = (sums[e] + got0[...]).astype(half.dtype)
     round1 = []
-    for k in range(1, chips):
-        other = lax.rem(chip + k, chips)
-        round1.append(
-            send(half.at[other], got1.at[k - 1], out1.at[k - 1], in1.at[k - 1], t, 2 * other + e)
-        )
-        round1[-1].start()
+    for n in range(pieces):
+        swap[n].wait_recv()
+        half[:, cut(n), :] = (sums[e, :, cut(n), :] + got0[:, cut(n), :]).astype(half.dtype)
+        for k in range(1, chips):
+            other = lax.rem(chip + k, chips)
+            round1.append(
+                send(
+                    half.at[other, cut(n)],
+                    got1.at[k - 1, cut(n)],
+                    out1.at[n, k - 1],
+                    in1.at[n, k - 1],
+                    t,
+                    2 * other + e,
+                )
+            )
+            round1[-1].start()
     both(1)
-    total = sums[e, chip] + got0[chip]
-    for k in range(1, chips):
-        round1[k - 1].wait_recv()
-        total = total + got1[k - 1].astype(jnp.float32)
-    for s in range(tilts):
-        plane[s] = total[s * 3 * chunk : (s + 1) * 3 * chunk]
-    round2 = []
-    for k in range(1, tilts):
-        other = lax.rem(t + k, tilts)
-        round2.append(
-            send(plane.at[other], got2.at[k - 1], out2.at[k - 1], in2.at[k - 1], other, p)
-        )
-        round2[-1].start()
+    for n in range(pieces):
+        total = sums[e, chip, cut(n)] + got0[chip, cut(n)]
+        for k in range(1, chips):
+            round1[n * (chips - 1) + k - 1].wait_recv()
+            total = total + got1[k - 1, cut(n)].astype(jnp.float32)
+        for s in range(per):
+            other = n * per + s
+            plane[other] = total[s * 3 * chunk : (s + 1) * 3 * chunk]
+
+            @pl.when(t != other)
+            def _(other=other):
+                k = lax.rem(other - t + tilts, tilts) - 1
+                send(plane.at[other], got2.at[k], out2.at[k], in2.at[k], other, p).start()
+
     both(2)
     total = plane[t]
     for k in range(1, tilts):
-        round2[k - 1].wait_recv()
+        send(plane.at[0], got2.at[k - 1], out2.at[k - 1], in2.at[k - 1], t, partner).wait_recv()
         total = total + got2[k - 1]
     below = total[2 * chunk :]
     column[...] = total[: 2 * chunk] / jnp.concatenate([below, below], 0)
@@ -671,33 +695,26 @@
             send(column, result.at[e, chip, t], out3.at[k - 1], in3.at[k - 1], other, p)
         )
         round3[-1].start()
-    for k in range(1, tilts):
-        round3[k - 1].wait_recv()
+    order = sorted(range(tilts), key=lambda m: min(m, tilts - m))
     round4 = []
-    for k in range(1, chips):
-        other = lax.rem(chip + k, chips)
-        round4.append(
-            send(
-                result.at[e, chip],
-                result.at[e, chip],
-                out4.at[k - 1],
-                in4.at[k - 1],
-                t,
-                2 * other + e,
+    for m in order:
+        whose = lax.rem(t - m + tilts, tilts)
+        if m > 0:
+            round3[m - 1].wait_recv()
+        for k in range(1, chips):
+            other = lax.rem(chip + k, chips)
+            round4.append(
+                send(
+                    result.at[e, chip, whose],
+                    result.at[e, chip, whose],
+                    out4.at[m, k - 1],
+                    in4.at[m, k - 1],
+                    t,
+                    2 * other + e,
+                )
             )
-        )
-        round4[-1].start()
-    for k in range(1, chips):
-        round4[k - 1].wait_recv()
-    back = send(result.at[e], result.at[e], out5.at[0], in5.at[0], t, partner)
-    back.start()
-
+            round4[-1].start()
     both(3)
-    for c in range(2):
-        for g in range(groups):
-            object_ref[0, c, :, g * LANES : (g + 1) * LANES] = (
-                grads[c, g, pl.ds(2 * rows, rows), :] + mine[c, g]
-            )
     for side, has, landed in [(0, chip > 0, from_left), (1, chip < chips - 1, from_right)]:
 
         @pl.when(has)
@@ -706,24 +723,22 @@
                 send(
                     near.at[c], landed.at[c], obj_out.at[1, c], obj_in.at[side, c], t, partner
                 ).wait_recv()
-                for g in range(groups):
-                    object_ref[0, c, :, g * LANES : (g + 1) * LANES] += landed[c, g].astype(
-                        jnp.float32
-                    )
-
-    back.wait_recv()
-    for i in range(2):
-        for c in range(chips):
-            for s in range(tilts):
-                start = ((i * chips + c) * tilts + s) * chunk
-                for k in range(2):
-                    probe_ref[k, start : start + chunk, :] = result[
-                        i, c, s, k * chunk : (k + 1) * chunk, :
-                    ]
-    swap.wait_send()
-    for copy in round1 + round2 + round3 + round4:
+
+    back = []
+    for n, m in enumerate(order):
+        whose = lax.rem(t - m + tilts, tilts)
+        for k in range(1, chips):
+            round4[n * (chips - 1) + k - 1].wait_recv()
+        back.append(
+            send(result.at[e, :, whose], result.at[e, :, whose], out5.at[m], in5.at[m], t, partner)
+        )
+        back[-1].start()
+    for copy in back:
+        copy.wait_recv()
+    for copy in swap + round1 + round3 + round4 + back:
         copy.wait_send()
-    back.wait_send()
+    for k in range(1, tilts):
+        send(plane.at[0], got2.at[k - 1], out2.at[k - 1], in2.at[k - 1], t, partner).wait_send()
 
 
 def exchange(tilts, devices, width, rows, grads, sums):
@@ -731,19 +746,22 @@
     planes, groups = grads.shape[0], grads.shape[1] - 1
     _, chips, part, _ = sums.shape
     third = part // tilts
+    pieces = 2 if tilts % 2 == 0 and part % 32 == 0 else 1
     block = (planes, groups, rows, LANES)
     dma = pltpu.SemaphoreType.DMA
     f32, bf16 = jnp.float32, jnp.bfloat16
     return pl.pallas_call(
         functools.partial(exchange_kernel, tilts, devices),
         out_shape=[
-            jax.ShapeDtypeStruct((1, planes, rows, groups * LANES), f32),
-            jax.ShapeDtypeStruct((2, width, width), f32),
+            pltpu.VMEM(block, f32),
+            pltpu.VMEM(block, bf16),
+            pltpu.VMEM(block, bf16),
+            pltpu.VMEM((2, chips, tilts, 2 * third // 3, width), f32),
         ],
         in_specs=[vmem] * 2,
-        out_specs=[vmem] * 2,
-        scratch_shapes=[pltpu.VMEM(block, f32)] * 2
-        + [pltpu.VMEM(block, bf16)] * 4
+        out_specs=[vmem] * 4,
+        scratch_shapes=[pltpu.VMEM(block, f32)]
+        + [pltpu.VMEM(block, bf16)] * 2
         + [
             pltpu.VMEM((2,) + block[1:], bf16),
             pltpu.VMEM((chips, part, width), bf16),
@@ -752,18 +770,73 @@
             pltpu.VMEM((tilts, third, width), f32),
             pltpu.VMEM((2 * third // 3, width), f32),
             pltpu.VMEM((tilts - 1, third, width), f32),
-            pltpu.VMEM((2, chips, tilts, 2 * third // 3, width), f32),
         ]
         + [dma((3, 2)), dma((3, 2)), dma((4,)), dma((2,))]
-        + [dma((1,))] * 2
-        + [dma((chips - 1,))] * 2
+        + [dma((pieces,))] * 2
+        + [dma((pieces, chips - 1))] * 2
         + [dma((tilts - 1,))] * 4
-        + [dma((chips - 1,))] * 2
-        + [dma((1,))] * 2,
+        + [dma((tilts, chips - 1))] * 2
+        + [dma((tilts,))] * 2,
         compiler_params=pltpu.CompilerParams(
             collective_id=2, has_side_effects=True, vmem_limit_bytes=20 * 1024 * 1024
         ),
     )(grads, sums)
+
+
+def finish_kernel(
+    devices, total, mine, left, right, result, object_any, probe_any, object_ref, probe_ref, sems
+):
+    p = lax.axis_index("pos")
+    has_left, has_right = p >= 2, p < devices - 2
+    groups, rows = mine.shape[1:3]
+    pairs, chips, tilts, part, _ = result.shape
+    chunk = part // 2
+    copies = []
+
+    def leave(src, dst):
+        copies.append(pltpu.make_async_copy(src, dst, sems.at[len(copies)]))
+        copies[-1].start()
+
+    for k in range(2):
+        for i in range(pairs):
+            for c in range(chips):
+                for s in range(tilts):
+                    start = ((i * chips + c) * tilts + s) * chunk
+                    probe_ref[k, start : start + chunk, :] = result[
+                        i, c, s, k * chunk : (k + 1) * chunk, :
+                    ]
+        leave(probe_ref.at[k], probe_any.at[k])
+    for c in range(2):
+        for g in range(groups):
+            object_ref[c, :, g * LANES : (g + 1) * LANES] = (
+                total[c, g, pl.ds(2 * rows, rows), :]
+                + mine[c, g]
+                + jnp.where(has_left, left[c, g].astype(jnp.float32), 0.0)
+                + jnp.where(has_right, right[c, g].astype(jnp.float32), 0.0)
+            )
+        leave(object_ref.at[c], object_any.at[0, c])
+    for copy in copies:
+        copy.wait()
+
+
+def finish(devices, width, total, mine, left, right, result):
+    planes, groups, rows, _ = mine.shape
+    vmem = pl.BlockSpec(memory_space=pltpu.VMEM)
+    hbm = pl.BlockSpec(memory_space=pltpu.HBM)
+    f32 = jnp.float32
+    shapes = [(planes, rows, groups * LANES), (2, width, width)]
+    return pl.pallas_call(
+        functools.partial(finish_kernel, devices),
+        out_shape=[
+            jax.ShapeDtypeStruct((1,) + shapes[0], f32),
+            jax.ShapeDtypeStruct(shapes[1], f32),
+        ],
+        in_specs=[vmem] * 5,
+        out_specs=[hbm] * 2,
+        scratch_shapes=[pltpu.VMEM(shape, f32) for shape in shapes]
+        + [pltpu.SemaphoreType.DMA((4,))],
+        compiler_params=pltpu.CompilerParams(vmem_limit_bytes=16 * 1024 * 1024),
+    )(total, mine, left, right, result)
 
 
 def local(tilts, devices, intensity, positions, counts, object_field, probe):
@@ -784,7 +857,8 @@
     grads, sums = frame_sums(
         reach, tilts, parts, places, counts, frames, band, probe_v, forward, inverse
     )
-    return tuple(exchange(tilts, devices, width, rows, grads, sums))
+    parts = exchange(tilts, devices, width, rows, grads, sums)
+    return tuple(finish(devices, width, grads, *parts))
 
 
 def solution(mesh):

time: 56.4 us -> 54.1 us (0.959)
  local copies, waits for them, and re-layouts: 1.61 us -> 0 us
  Pallas kernels: 53.6 us -> 52.3 us
    pallas_call x1, Pallas kernels: 16 us -> 13.3 us  [gather(): pl.pallas_call(functools.partial(gather_kernel, devices), out_shape=[pltp...]
    unnamed x2 -> x0, local copies, waits for them, and re-layouts: 1.61 us -> none
    pallas_call x0 -> x1, Pallas kernels: none -> 1.04 us  [finish(): pl.pallas_call(functools.partial(finish_kernel, devices), out_shape=[jax....]
where the time goes in v4:
time: 54.1 us; the launch traced here: 53.6 us
  Pallas kernels  52.3 us (97%)
  between operations  1.3 us (2%)
    pallas_call x1, Pallas kernels, exchange(): pl.pallas_call(functools.partial(exchange_kernel, tilts, devices), out_sh...  31.4 us
    pallas_call x1, Pallas kernels, gather(): pl.pallas_call(functools.partial(gather_kernel, devices), out_shape=[pltp...  13.3 us
    pallas_call x1, Pallas kernels, frame_sums(): pl.pallas_call(functools.partial(frames_kernel, reach, tilts), out_shape=...  6.65 us

profile of v4, /device:TPU:0, one launch (start us, length us, event | category | flops | bytes accessed | tf_op | source)
XLA Modules:
  0.0 53.6 jit_solution(15855637716310781372)
XLA Ops:
  1.3 13.3 %shard_map.95 = (f32[2,7,480,128]{3,2,1,0:T(8,128)S(1)}, bf16[16,256,256]{2,1,0:T(8,128)(2,1)S(1)}, f32[2,256,256]{2,1,0:T(8,128)S(1)}, bf16[1024,256]{1,0:T(8,1...) custom-call(bf16[1,2,96,768]{3,2,1,0:T(8,128)(2,1)} %field_any.1, bf16[1,16,256,256]{3,2,1,0:T(8,128)(2,1)} %frames_any.1, ...), custom_call_target="tpu_custom_call" | custom-call | tf_op jit(solution)/shard_map/pallas_call | solution.py:500
  14.6 6.7 %shard_map.96 = (f32[2,7,480,128]{3,2,1,0:T(8,128)S(1)}, f32[2,4,96,256]{3,2,1,0:T(8,128)S(1)}) custom-call(s32[2,16]{1,0:T(2,128)S(1)} %get-tuple-element.14.pos_any, s32[1,1]{1,0:T(1,128)S(6)} %copy.10.count_ref, bf16[16,256,256]{2,1,0:T(8,128)(2,1)S(1)} %get-tuple-element.15.frames_ref, f32[2,7,480,128]{3,2,1,0:T(8,128)S(1)} %get-tuple-element.16.band, ...), custom_call_target="tpu_custom_call" | custom-call | tf_op jit(solution)/shard_map/pallas_call | solution.py:258
  21.2 31.4 %shard_map.97 = (f32[2,6,96,128]{3,2,1,0:T(8,128)S(1)}, bf16[2,6,96,128]{3,2,1,0:T(8,128)(2,1)S(1)}, bf16[2,6,96,128]{3,2,1,0:T(8,128)(2,1)S(1)}, f32[2,4,4,16,256]{4,3,2,1,0:T(8,128)S(1)}) custom-call(f32[2,7,480,128]{3,2,1,0:T(8,128)S(1)} %get-tuple-element.20.refs_0_.total, f32[2,4,96,256]{3,2,1,0:T(8,128)S(1)} %get-tuple-element.21.refs_1_), custom_call_target="tpu_custom_call" | custom-call | tf_op jit(solution)/shard_map/pallas_call | solution.py:753
  52.6 1.0 %shard_map.98 = (f32[1,2,96,768]{3,2,1,0:T(8,128)}, f32[2,256,256]{2,1,0:T(8,128)}) custom-call(f32[2,7,480,128]{3,2,1,0:T(8,128)S(1)} %get-tuple-element.20.refs_0_.total, f32[2,6,96,128]{3,2,1,0:T(8,128)S(1)} %get-tuple-element.22.mine, bf16[2,6,96,128]{3,2,1,0:T(8,128)(2,1)S(1)} %get-tuple-element.23.left, ...), custom_call_target="tpu_custom_call" | custom-call | tf_op jit(solution)/shard_map/pallas_call | solution.py:828

commit v5 on v4

--- a/solution.py
+++ b/solution.py
@@ -593,13 +593,14 @@
             b = 4 if odd else 0
             for c in range(2):
                 distant[c] = grads[c, 0:groups, pl.ds(b * rows, rows), :].astype(distant.dtype)
-            pl.when(has)(far[0].start)
             if relay:
                 pl.when(middle)(up[0].start)
         elif step == 1:
             if relay:
+                pl.when(has)(far[0].start)
                 pl.when(has & ~middle)(far[1].start)
             else:
+                pl.when(has)(far[0].start)
                 pl.when(has)(far[1].start)
             to_mine.start()
             to_extra.wait_recv()

time: 54.1 us -> 53.2 us (0.983)
    pallas_call x1, Pallas kernels: 31.4 us -> 30.8 us  [exchange(): pl.pallas_call(functools.partial(exchange_kernel, tilts, devices), out_sh...]
where the time goes in v5:
time: 53.2 us; the launch traced here: 53.1 us
  Pallas kernels  51.8 us (97%)
  between operations  1.3 us (2%)
    pallas_call x1, Pallas kernels, exchange(): pl.pallas_call(functools.partial(exchange_kernel, tilts, devices), out_sh...  30.8 us
    pallas_call x1, Pallas kernels, gather(): pl.pallas_call(functools.partial(gather_kernel, devices), out_shape=[pltp...  13.3 us
    pallas_call x1, Pallas kernels, frame_sums(): pl.pallas_call(functools.partial(frames_kernel, reach, tilts), out_shape=...  6.65 us

profile of v5, /device:TPU:0, one launch (start us, length us, event | category | flops | bytes accessed | tf_op | source)
XLA Modules:
  0.0 53.1 jit_solution(1174718312978041447)
XLA Ops:
  1.3 13.3 %shard_map.95 = (f32[2,7,480,128]{3,2,1,0:T(8,128)S(1)}, bf16[16,256,256]{2,1,0:T(8,128)(2,1)S(1)}, f32[2,256,256]{2,1,0:T(8,128)S(1)}, bf16[1024,256]{1,0:T(8,1...) custom-call(bf16[1,2,96,768]{3,2,1,0:T(8,128)(2,1)} %field_any.1, bf16[1,16,256,256]{3,2,1,0:T(8,128)(2,1)} %frames_any.1, ...), custom_call_target="tpu_custom_call" | custom-call | tf_op jit(solution)/shard_map/pallas_call | solution.py:500
  14.6 6.6 %shard_map.96 = (f32[2,7,480,128]{3,2,1,0:T(8,128)S(1)}, f32[2,4,96,256]{3,2,1,0:T(8,128)S(1)}) custom-call(s32[2,16]{1,0:T(2,128)S(1)} %get-tuple-element.14.pos_any, s32[1,1]{1,0:T(1,128)S(6)} %copy.10.count_ref, bf16[16,256,256]{2,1,0:T(8,128)(2,1)S(1)} %get-tuple-element.15.frames_ref, f32[2,7,480,128]{3,2,1,0:T(8,128)S(1)} %get-tuple-element.16.band, ...), custom_call_target="tpu_custom_call" | custom-call | tf_op jit(solution)/shard_map/pallas_call | solution.py:258
  21.2 30.8 %shard_map.97 = (f32[2,6,96,128]{3,2,1,0:T(8,128)S(1)}, bf16[2,6,96,128]{3,2,1,0:T(8,128)(2,1)S(1)}, bf16[2,6,96,128]{3,2,1,0:T(8,128)(2,1)S(1)}, f32[2,4,4,16,256]{4,3,2,1,0:T(8,128)S(1)}) custom-call(f32[2,7,480,128]{3,2,1,0:T(8,128)S(1)} %get-tuple-element.20.refs_0_.total, f32[2,4,96,256]{3,2,1,0:T(8,128)S(1)} %get-tuple-element.21.refs_1_), custom_call_target="tpu_custom_call" | custom-call | tf_op jit(solution)/shard_map/pallas_call | solution.py:754
  52.1 1.0 %shard_map.98 = (f32[1,2,96,768]{3,2,1,0:T(8,128)}, f32[2,256,256]{2,1,0:T(8,128)}) custom-call(f32[2,7,480,128]{3,2,1,0:T(8,128)S(1)} %get-tuple-element.20.refs_0_.total, f32[2,6,96,128]{3,2,1,0:T(8,128)S(1)} %get-tuple-element.22.mine, bf16[2,6,96,128]{3,2,1,0:T(8,128)(2,1)S(1)} %get-tuple-element.23.left, ...), custom_call_target="tpu_custom_call" | custom-call | tf_op jit(solution)/shard_map/pallas_call | solution.py:829

commit v6 on v5

--- a/solution.py
+++ b/solution.py
@@ -74,6 +74,8 @@
     probe_ref,
     fwd_ref,
     inv_ref,
+    clear_total,
+    clear_sums,
     total,
     chunks_ref,
     sums_ref,
@@ -87,8 +89,6 @@
     width = probe_ref.shape[-1]
     wide = width // LANES
 
-    total[...] = jnp.zeros_like(total)
-    sums_ref[...] = jnp.zeros_like(sums_ref)
     first = (lax.axis_index("pos") - reach) * rows
     fetch.wait()
 
@@ -252,7 +252,9 @@
                     ]
 
 
-def frame_sums(reach, tilts, parts, positions, count, frames, band, probe, forward, inverse):
+def frame_sums(
+    reach, tilts, parts, positions, count, frames, band, probe, forward, inverse, total, sums
+):
     vmem = pl.BlockSpec(memory_space=pltpu.VMEM)
     smem = pl.BlockSpec(memory_space=pltpu.SMEM)
     return pl.pallas_call(
@@ -260,17 +262,18 @@
         out_shape=[
             jax.ShapeDtypeStruct(band.shape, jnp.float32),
             jax.ShapeDtypeStruct(parts, jnp.float32),
+            jax.ShapeDtypeStruct(sums.shape, jnp.float32),
         ],
-        in_specs=[vmem, smem] + [vmem] * 5,
-        out_specs=[vmem] * 2,
+        in_specs=[vmem, smem] + [vmem] * 7,
+        out_specs=[vmem] * 3,
+        input_output_aliases={7: 0, 8: 2},
         scratch_shapes=[
-            pltpu.VMEM((3,) + probe.shape[1:], jnp.float32),
             pltpu.VMEM((GROUP, 2) + probe.shape[1:], jnp.float32),
             pltpu.SMEM(positions.shape, jnp.int32),
             pltpu.SemaphoreType.DMA,
         ],
         compiler_params=pltpu.CompilerParams(vmem_limit_bytes=24 * 1024 * 1024),
-    )(positions, count, frames, band, probe, forward, inverse)
+    )(positions, count, frames, band, probe, forward, inverse, total, sums)[:2]
 
 
 def greet(tilts, devices):
@@ -323,6 +326,8 @@
     fwd_ref,
     inv_ref,
     pos_ref,
+    total,
+    sums_ref,
     own,
     slots,
     stage,
@@ -443,6 +448,8 @@
         for c in range(2):
             band[c, groups] = jnp.zeros(band.shape[2:], jnp.float32)
         place(own, 2)
+        total[...] = jnp.zeros_like(total)
+        sums_ref[...] = jnp.zeros_like(sums_ref)
         for c in range(2):
             arrived(from_partner, c)
         place(slots.at[from_partner], from_partner)
@@ -494,7 +501,7 @@
     block = (planes, rows, columns)
     groups = columns // LANES
     dma = pltpu.SemaphoreType.DMA
-    held = 4 * planes * (groups + 1) * 5 * rows * LANES + sum(
+    held = 8 * planes * (groups + 1) * 5 * rows * LANES + 6 * probe.size + sum(
         a.size * a.dtype.itemsize for a in (frames, probe, forward, inverse)
     )
     return pl.pallas_call(
@@ -506,9 +513,11 @@
             pltpu.VMEM(forward.shape, forward.dtype),
             pltpu.VMEM(inverse.shape, inverse.dtype),
             pltpu.VMEM(positions.shape, positions.dtype),
+            pltpu.VMEM((planes, groups + 1, 5 * rows, LANES), jnp.float32),
+            pltpu.VMEM((3,) + probe.shape[1:], jnp.float32),
         ],
         in_specs=[hbm] * 7,
-        out_specs=[vmem] * 6,
+        out_specs=[vmem] * 8,
         scratch_shapes=[
             pltpu.VMEM(block, field.dtype),
             pltpu.VMEM((5,) + block, field.dtype),
@@ -851,12 +860,23 @@
     moves = jnp.asarray(
         np.stack([identity[row_order], identity[column_order].T]).astype(ml_dtypes.bfloat16)
     )
-    band, frames, probe_v, forward, inverse, places = gather(
+    band, frames, probe_v, forward, inverse, places, total, sums = gather(
         devices, object_field, intensity, probe, forward, inverse, positions[0].T, moves
     )
     parts = (2, devices // 2, 3 * width // devices, width)
     grads, sums = frame_sums(
-        reach, tilts, parts, places, counts, frames, band, probe_v, forward, inverse
+        reach,
+        tilts,
+        parts,
+        places,
+        counts,
+        frames,
+        band,
+        probe_v,
+        forward,
+        inverse,
+        total,
+        sums,
     )
     parts = exchange(tilts, devices, width, rows, grads, sums)
     return tuple(finish(devices, width, grads, *parts))

time: 53.2 us -> 53.6 us (level); the launches traced: 53.1 us -> 52.7 us
    pallas_call x1, Pallas kernels: 30.8 us -> 30.1 us  [exchange(): pl.pallas_call(functools.partial(exchange_kernel, tilts, devices), out_sh...]
where the time goes in v6:
time: 53.6 us; the launch traced here: 52.7 us
  Pallas kernels  51.4 us (96%)
  between operations  1.3 us (2%)
    pallas_call x1, Pallas kernels, exchange(): pl.pallas_call(functools.partial(exchange_kernel, tilts, devices), out_sh...  30.1 us
    pallas_call x1, Pallas kernels, gather(): pl.pallas_call(functools.partial(gather_kernel, devices), out_shape=[pltp...  13.3 us
    pallas_call x1, Pallas kernels, frame_sums(): pl.pallas_call(functools.partial(frames_kernel, reach, tilts), out_shape=...  7 us

profile of v6, /device:TPU:0, one launch (start us, length us, event | category | flops | bytes accessed | tf_op | source)
XLA Modules:
  0.0 52.7 jit_solution(1228196974142583628)
XLA Ops:
  1.3 13.3 %shard_map.95 = (f32[2,7,480,128]{3,2,1,0:T(8,128)S(1)}, bf16[16,256,256]{2,1,0:T(8,128)(2,1)S(1)}, f32[2,256,256]{2,1,0:T(8,128)S(1)}, bf16[1024,256]{1,0:T(8,1...) custom-call(bf16[1,2,96,768]{3,2,1,0:T(8,128)(2,1)} %field_any.1, ...), custom_call_target="tpu_custom_call" | custom-call | tf_op jit(solution)/shard_map/pallas_call | solution.py:507
  14.6 7.0 %shard_map.96 = (f32[2,7,480,128]{3,2,1,0:T(8,128)S(1)}, f32[2,4,96,256]{3,2,1,0:T(8,128)S(1)}, f32[3,256,256]{2,1,0:T(8,128)S(1)}) custom-call(s32[2,16]{1,0:T(2,128)S(1)} %get-tuple-element.16.pos_any, s32[1,1]{1,0:T(1,128)S(6)} %copy.14.count_ref, ...), custom_call_target="tpu_custom_call", output_to_operand_aliasing={{0}: (7, {}), {2}: (8, {})} | custom-call | tf_op jit(solution)/shard_map/pallas_call | solution.py:260
  21.6 30.1 %shard_map.97 = (f32[2,6,96,128]{3,2,1,0:T(8,128)S(1)}, bf16[2,6,96,128]{3,2,1,0:T(8,128)(2,1)S(1)}, bf16[2,6,96,128]{3,2,1,0:T(8,128)(2,1)S(1)}, f32[2,4,4,16,256]{4,3,2,1,0:T(8,128)S(1)}) custom-call(f32[2,7,480,128]{3,2,1,0:T(8,128)S(1)} %get-tuple-element.24.refs_0_.total, f32[2,4,96,256]{3,2,1,0:T(8,128)S(1)} %get-tuple-element.25.refs_1_), custom_call_target="tpu_custom_call" | custom-call | tf_op jit(solution)/shard_map/pallas_call | solution.py:763
  51.7 1.0 %shard_map.98 = (f32[1,2,96,768]{3,2,1,0:T(8,128)}, f32[2,256,256]{2,1,0:T(8,128)}) custom-call(f32[2,7,480,128]{3,2,1,0:T(8,128)S(1)} %get-tuple-element.24.refs_0_.total, f32[2,6,96,128]{3,2,1,0:T(8,128)S(1)} %get-tuple-element.26.mine, bf16[2,6,96,128]{3,2,1,0:T(8,128)(2,1)S(1)} %get-tuple-element.27.left, ...), custom_call_target="tpu_custom_call" | custom-call | tf_op jit(solution)/shard_map/pallas_call | solution.py:838

commit v7 on v5

--- a/solution.py
+++ b/solution.py
@@ -612,21 +612,21 @@
             pl.when(has)(close[0].start)
             if relay:
                 pl.when(middle)(up[1].start)
-                pl.when(has & ~middle)(close[1].start)
 
                 @pl.when(corner)
                 def _():
                     up[0].wait_recv()
                     on[0].start()
-            else:
-                pl.when(has)(close[1].start)
         elif step == 2:
             if relay:
+                pl.when(has & ~middle)(close[1].start)
 
                 @pl.when(corner)
                 def _():
                     up[1].wait_recv()
                     on[1].start()
+            else:
+                pl.when(has)(close[1].start)
         else:
             to_mine.wait_recv()
             to_extra.wait_send()
@@ -681,7 +681,6 @@
                 k = lax.rem(other - t + tilts, tilts) - 1
                 send(plane.at[other], got2.at[k], out2.at[k], in2.at[k], other, p).start()
 
-    both(2)
     total = plane[t]
     for k in range(1, tilts):
         send(plane.at[0], got2.at[k - 1], out2.at[k - 1], in2.at[k - 1], t, partner).wait_recv()
@@ -715,16 +714,7 @@
                 )
             )
             round4[-1].start()
-    both(3)
-    for side, has, landed in [(0, chip > 0, from_left), (1, chip < chips - 1, from_right)]:
-
-        @pl.when(has)
-        def _():
-            for c in range(2):
-                send(
-                    near.at[c], landed.at[c], obj_out.at[1, c], obj_in.at[side, c], t, partner
-                ).wait_recv()
-
+    both(2)
     back = []
     for n, m in enumerate(order):
         whose = lax.rem(t - m + tilts, tilts)
@@ -734,6 +724,16 @@
             send(result.at[e, :, whose], result.at[e, :, whose], out5.at[m], in5.at[m], t, partner)
         )
         back[-1].start()
+    both(3)
+    for side, has, landed in [(0, chip > 0, from_left), (1, chip < chips - 1, from_right)]:
+
+        @pl.when(has)
+        def _():
+            for c in range(2):
+                send(
+                    near.at[c], landed.at[c], obj_out.at[1, c], obj_in.at[side, c], t, partner
+                ).wait_recv()
+
     for copy in back:
         copy.wait_recv()
     for copy in swap + round1 + round3 + round4 + back:

time: 53.2 us -> 53.9 us (1.013)
    pallas_call x1, Pallas kernels: 30.8 us -> 31.4 us  [exchange(): pl.pallas_call(functools.partial(exchange_kernel, tilts, devices), out_sh...]
where the time goes in v7:
time: 53.9 us; the launch traced here: 53.6 us
  Pallas kernels  52.3 us (97%)
  between operations  1.3 us (2%)
    pallas_call x1, Pallas kernels, exchange(): pl.pallas_call(functools.partial(exchange_kernel, tilts, devices), out_sh...  31.4 us
    pallas_call x1, Pallas kernels, gather(): pl.pallas_call(functools.partial(gather_kernel, devices), out_shape=[pltp...  13.3 us
    pallas_call x1, Pallas kernels, frame_sums(): pl.pallas_call(functools.partial(frames_kernel, reach, tilts), out_shape=...  6.62 us

profile of v7, /device:TPU:0, one launch (start us, length us, event | category | flops | bytes accessed | tf_op | source)
XLA Modules:
  0.0 53.6 jit_solution(2810374646470492907)
XLA Ops:
  1.3 13.3 %shard_map.95 = (f32[2,7,480,128]{3,2,1,0:T(8,128)S(1)}, bf16[16,256,256]{2,1,0:T(8,128)(2,1)S(1)}, f32[2,256,256]{2,1,0:T(8,128)S(1)}, bf16[1024,256]{1,0:T(8,1...) custom-call(bf16[1,2,96,768]{3,2,1,0:T(8,128)(2,1)} %field_any.1, bf16[1,16,256,256]{3,2,1,0:T(8,128)(2,1)} %frames_any.1, ...), custom_call_target="tpu_custom_call" | custom-call | tf_op jit(solution)/shard_map/pallas_call | solution.py:500
  14.6 6.6 %shard_map.96 = (f32[2,7,480,128]{3,2,1,0:T(8,128)S(1)}, f32[2,4,96,256]{3,2,1,0:T(8,128)S(1)}) custom-call(s32[2,16]{1,0:T(2,128)S(1)} %get-tuple-element.14.pos_any, s32[1,1]{1,0:T(1,128)S(6)} %copy.10.count_ref, bf16[16,256,256]{2,1,0:T(8,128)(2,1)S(1)} %get-tuple-element.15.frames_ref, f32[2,7,480,128]{3,2,1,0:T(8,128)S(1)} %get-tuple-element.16.band, ...), custom_call_target="tpu_custom_call" | custom-call | tf_op jit(solution)/shard_map/pallas_call | solution.py:258
  21.2 31.4 %shard_map.97 = (f32[2,6,96,128]{3,2,1,0:T(8,128)S(1)}, bf16[2,6,96,128]{3,2,1,0:T(8,128)(2,1)S(1)}, bf16[2,6,96,128]{3,2,1,0:T(8,128)(2,1)S(1)}, f32[2,4,4,16,256]{4,3,2,1,0:T(8,128)S(1)}) custom-call(f32[2,7,480,128]{3,2,1,0:T(8,128)S(1)} %get-tuple-element.20.refs_0_.total, f32[2,4,96,256]{3,2,1,0:T(8,128)S(1)} %get-tuple-element.21.refs_1_), custom_call_target="tpu_custom_call" | custom-call | tf_op jit(solution)/shard_map/pallas_call | solution.py:754
  52.6 1.0 %shard_map.98 = (f32[1,2,96,768]{3,2,1,0:T(8,128)}, f32[2,256,256]{2,1,0:T(8,128)}) custom-call(f32[2,7,480,128]{3,2,1,0:T(8,128)S(1)} %get-tuple-element.20.refs_0_.total, f32[2,6,96,128]{3,2,1,0:T(8,128)S(1)} %get-tuple-element.22.mine, bf16[2,6,96,128]{3,2,1,0:T(8,128)(2,1)S(1)} %get-tuple-element.23.left, ...), custom_call_target="tpu_custom_call" | custom-call | tf_op jit(solution)/shard_map/pallas_call | solution.py:829

commit v8 on v7

--- a/solution.py
+++ b/solution.py
@@ -273,7 +273,7 @@
     )(positions, count, frames, band, probe, forward, inverse)
 
 
-def greet(tilts, devices):
+def greet(tilts, devices, meanwhile=lambda: None):
     t, p = lax.axis_index("tilt"), lax.axis_index("pos")
     barrier = pltpu.get_barrier_semaphore()
     for k in range(1, devices):
@@ -290,6 +290,7 @@
             device_id=(lax.rem(t + k, tilts), p),
             device_id_type=pl.DeviceIdType.MESH,
         )
+    meanwhile()
     pl.semaphore_wait(barrier, devices - 1 + tilts - 1)
 
 
@@ -530,9 +531,9 @@
 def exchange_kernel(tilts, devices, *refs):
     grads, sums, mine, from_left, from_right, result = refs[:6]
     extra, near, distant, stage = refs[6:10]
-    half, got0, got1, plane, column, got2 = refs[10:16]
-    obj_out, obj_in, stage_out, stage_in = refs[16:20]
-    out0, in0, out1, in1, out2, in2, out3, in3, out4, in4, out5, in5 = refs[20:]
+    half, got0, got1, plane, column, got2, given = refs[10:17]
+    obj_out, obj_in, stage_out, stage_in = refs[17:21]
+    out0, in0, out1, in1, out2, in2, out3, in3, out4, in4, out5, in5 = refs[21:]
     t, p = lax.axis_index("tilt"), lax.axis_index("pos")
     chip, chips = p // 2, devices // 2
     e = lax.rem(p, 2)
@@ -540,7 +541,11 @@
     groups, rows = mine.shape[1:3]
     chunk = column.shape[0] // 2
     relay = relayed(devices)
-    greet(tilts, devices)
+
+    def meanwhile():
+        given[...] = sums[1 - e].astype(given.dtype)
+
+    greet(tilts, devices, meanwhile)
 
     def block(b):
         return grads.at[:, pl.ds(0, groups), pl.ds(b * rows, rows), :]
@@ -555,7 +560,7 @@
 
     swap = [
         send(
-            sums.at[1 - e, :, cut(n), :], got0.at[:, cut(n), :], out0.at[n], in0.at[n], t, partner
+            given.at[:, cut(n), :], got0.at[:, cut(n), :], out0.at[n], in0.at[n], t, partner
         )
         for n in range(pieces)
     ]
@@ -652,7 +657,9 @@
     round1 = []
     for n in range(pieces):
         swap[n].wait_recv()
-        half[:, cut(n), :] = (sums[e, :, cut(n), :] + got0[:, cut(n), :]).astype(half.dtype)
+        half[:, cut(n), :] = (
+            sums[e, :, cut(n), :] + got0[:, cut(n), :].astype(jnp.float32)
+        ).astype(half.dtype)
         for k in range(1, chips):
             other = lax.rem(chip + k, chips)
             round1.append(
@@ -668,7 +675,7 @@
             round1[-1].start()
     both(1)
     for n in range(pieces):
-        total = sums[e, chip, cut(n)] + got0[chip, cut(n)]
+        total = sums[e, chip, cut(n)] + got0[chip, cut(n)].astype(jnp.float32)
         for k in range(1, chips):
             round1[n * (chips - 1) + k - 1].wait_recv()
             total = total + got1[k - 1, cut(n)].astype(jnp.float32)
@@ -766,11 +773,12 @@
         + [
             pltpu.VMEM((2,) + block[1:], bf16),
             pltpu.VMEM((chips, part, width), bf16),
-            pltpu.VMEM((chips, part, width), f32),
+            pltpu.VMEM((chips, part, width), bf16),
             pltpu.VMEM((chips - 1, part, width), bf16),
             pltpu.VMEM((tilts, third, width), f32),
             pltpu.VMEM((2 * third // 3, width), f32),
             pltpu.VMEM((tilts - 1, third, width), f32),
+            pltpu.VMEM((chips, part, width), bf16),
         ]
         + [dma((3, 2)), dma((3, 2)), dma((4,)), dma((2,))]
         + [dma((pieces,))] * 2

time: 53.9 us -> 53.3 us (0.989)
  no operation moved by 1% of the time
where the time goes in v8:
time: 53.3 us
  Pallas kernels  52 us (98%)
  between operations  1.3 us (2%)
    pallas_call x1, Pallas kernels, exchange(): pl.pallas_call(functools.partial(exchange_kernel, tilts, devices), out_sh...  31 us
    pallas_call x1, Pallas kernels, gather(): pl.pallas_call(functools.partial(gather_kernel, devices), out_shape=[pltp...  13.3 us
    pallas_call x1, Pallas kernels, frame_sums(): pl.pallas_call(functools.partial(frames_kernel, reach, tilts), out_shape=...  6.65 us

profile of v8, /device:TPU:0, one launch (start us, length us, event | category | flops | bytes accessed | tf_op | source)
XLA Modules:
  0.0 53.3 jit_solution(2579600864021043200)
XLA Ops:
  1.3 13.3 %shard_map.95 = (f32[2,7,480,128]{3,2,1,0:T(8,128)S(1)}, bf16[16,256,256]{2,1,0:T(8,128)(2,1)S(1)}, f32[2,256,256]{2,1,0:T(8,128)S(1)}, bf16[1024,256]{1,0:T(8,1...) custom-call(bf16[1,2,96,768]{3,2,1,0:T(8,128)(2,1)} %field_any.1, bf16[1,16,256,256]{3,2,1,0:T(8,128)(2,1)} %frames_any.1, ...), custom_call_target="tpu_custom_call" | custom-call | tf_op jit(solution)/shard_map/pallas_call | solution.py:501
  14.6 6.7 %shard_map.96 = (f32[2,7,480,128]{3,2,1,0:T(8,128)S(1)}, f32[2,4,96,256]{3,2,1,0:T(8,128)S(1)}) custom-call(s32[2,16]{1,0:T(2,128)S(1)} %get-tuple-element.14.pos_any, s32[1,1]{1,0:T(1,128)S(6)} %copy.10.count_ref, bf16[16,256,256]{2,1,0:T(8,128)(2,1)S(1)} %get-tuple-element.15.frames_ref, f32[2,7,480,128]{3,2,1,0:T(8,128)S(1)} %get-tuple-element.16.band, ...), custom_call_target="tpu_custom_call" | custom-call | tf_op jit(solution)/shard_map/pallas_call | solution.py:258
  21.2 31.0 %shard_map.97 = (f32[2,6,96,128]{3,2,1,0:T(8,128)S(1)}, bf16[2,6,96,128]{3,2,1,0:T(8,128)(2,1)S(1)}, bf16[2,6,96,128]{3,2,1,0:T(8,128)(2,1)S(1)}, f32[2,4,4,16,256]{4,3,2,1,0:T(8,128)S(1)}) custom-call(f32[2,7,480,128]{3,2,1,0:T(8,128)S(1)} %get-tuple-element.20.refs_0_.total, f32[2,4,96,256]{3,2,1,0:T(8,128)S(1)} %get-tuple-element.21.refs_1_), custom_call_target="tpu_custom_call" | custom-call | tf_op jit(solution)/shard_map/pallas_call | solution.py:761
  52.3 1.0 %shard_map.98 = (f32[1,2,96,768]{3,2,1,0:T(8,128)}, f32[2,256,256]{2,1,0:T(8,128)}) custom-call(f32[2,7,480,128]{3,2,1,0:T(8,128)S(1)} %get-tuple-element.20.refs_0_.total, f32[2,6,96,128]{3,2,1,0:T(8,128)S(1)} %get-tuple-element.22.mine, bf16[2,6,96,128]{3,2,1,0:T(8,128)(2,1)S(1)} %get-tuple-element.23.left, ...), custom_call_target="tpu_custom_call" | custom-call | tf_op jit(solution)/shard_map/pallas_call | solution.py:837

commit v9 on v7

--- a/solution.py
+++ b/solution.py
@@ -273,7 +273,7 @@
     )(positions, count, frames, band, probe, forward, inverse)
 
 
-def greet(tilts, devices):
+def greet(tilts, devices, meanwhile=lambda: None):
     t, p = lax.axis_index("tilt"), lax.axis_index("pos")
     barrier = pltpu.get_barrier_semaphore()
     for k in range(1, devices):
@@ -290,6 +290,7 @@
             device_id=(lax.rem(t + k, tilts), p),
             device_id_type=pl.DeviceIdType.MESH,
         )
+    meanwhile()
     pl.semaphore_wait(barrier, devices - 1 + tilts - 1)
 
 
@@ -540,7 +541,13 @@
     groups, rows = mine.shape[1:3]
     chunk = column.shape[0] // 2
     relay = relayed(devices)
-    greet(tilts, devices)
+
+    def meanwhile():
+        start = pl.multiple_of(4 * rows * e, 8)
+        for c in range(2):
+            distant[c] = grads[c, 0:groups, pl.ds(start, rows), :].astype(distant.dtype)
+
+    greet(tilts, devices, meanwhile)
 
     def block(b):
         return grads.at[:, pl.ds(0, groups), pl.ds(b * rows, rows), :]
@@ -590,9 +597,6 @@
             ]
         if step == 0:
             to_extra.start()
-            b = 4 if odd else 0
-            for c in range(2):
-                distant[c] = grads[c, 0:groups, pl.ds(b * rows, rows), :].astype(distant.dtype)
             if relay:
                 pl.when(middle)(up[0].start)
         elif step == 1:

time: 53.9 us -> 53.2 us (0.987); the launches traced: 53.6 us -> 53.5 us
  no operation moved by 1% of the time
where the time goes in v9:
time: 53.2 us; the launch traced here: 53.5 us
  Pallas kernels  52.2 us (98%)
  between operations  1.3 us (2%)
    pallas_call x1, Pallas kernels, exchange(): pl.pallas_call(functools.partial(exchange_kernel, tilts, devices), out_sh...  31.2 us
    pallas_call x1, Pallas kernels, gather(): pl.pallas_call(functools.partial(gather_kernel, devices), out_shape=[pltp...  13.3 us
    pallas_call x1, Pallas kernels, frame_sums(): pl.pallas_call(functools.partial(frames_kernel, reach, tilts), out_shape=...  6.66 us

profile of v9, /device:TPU:0, one launch (start us, length us, event | category | flops | bytes accessed | tf_op | source)
XLA Modules:
  0.0 53.5 jit_solution(4515565369557186242)
XLA Ops:
  1.3 13.3 %shard_map.95 = (f32[2,7,480,128]{3,2,1,0:T(8,128)S(1)}, bf16[16,256,256]{2,1,0:T(8,128)(2,1)S(1)}, f32[2,256,256]{2,1,0:T(8,128)S(1)}, bf16[1024,256]{1,0:T(8,1...) custom-call(bf16[1,2,96,768]{3,2,1,0:T(8,128)(2,1)} %field_any.1, bf16[1,16,256,256]{3,2,1,0:T(8,128)(2,1)} %frames_any.1, ...), custom_call_target="tpu_custom_call" | custom-call | tf_op jit(solution)/shard_map/pallas_call | solution.py:501
  14.6 6.7 %shard_map.96 = (f32[2,7,480,128]{3,2,1,0:T(8,128)S(1)}, f32[2,4,96,256]{3,2,1,0:T(8,128)S(1)}) custom-call(s32[2,16]{1,0:T(2,128)S(1)} %get-tuple-element.14.pos_any, s32[1,1]{1,0:T(1,128)S(6)} %copy.10.count_ref, bf16[16,256,256]{2,1,0:T(8,128)(2,1)S(1)} %get-tuple-element.15.frames_ref, f32[2,7,480,128]{3,2,1,0:T(8,128)S(1)} %get-tuple-element.16.band, ...), custom_call_target="tpu_custom_call" | custom-call | tf_op jit(solution)/shard_map/pallas_call | solution.py:258
  21.3 31.2 %shard_map.97 = (f32[2,6,96,128]{3,2,1,0:T(8,128)S(1)}, bf16[2,6,96,128]{3,2,1,0:T(8,128)(2,1)S(1)}, bf16[2,6,96,128]{3,2,1,0:T(8,128)(2,1)S(1)}, f32[2,4,4,16,256]{4,3,2,1,0:T(8,128)S(1)}) custom-call(f32[2,7,480,128]{3,2,1,0:T(8,128)S(1)} %get-tuple-element.20.refs_0_.total, f32[2,4,96,256]{3,2,1,0:T(8,128)S(1)} %get-tuple-element.21.refs_1_), custom_call_target="tpu_custom_call" | custom-call | tf_op jit(solution)/shard_map/pallas_call | solution.py:758
  52.4 1.0 %shard_map.98 = (f32[1,2,96,768]{3,2,1,0:T(8,128)}, f32[2,256,256]{2,1,0:T(8,128)}) custom-call(f32[2,7,480,128]{3,2,1,0:T(8,128)S(1)} %get-tuple-element.20.refs_0_.total, f32[2,6,96,128]{3,2,1,0:T(8,128)S(1)} %get-tuple-element.22.mine, bf16[2,6,96,128]{3,2,1,0:T(8,128)(2,1)S(1)} %get-tuple-element.23.left, ...), custom_call_target="tpu_custom_call" | custom-call | tf_op jit(solution)/shard_map/pallas_call | solution.py:833
